TPU v7x, 32 devices: a whole 2x2x4 slice. The times are simulated.
32 devices in a mesh: dom: 32 (over z, y, x, core).
Axes of the slice: x: 2, y: 2, z: 4, core: 2. Of those that a mesh axis runs over, the one named last changes fastest.
Arguments:
- elevation: float32 [8192, 128], P('dom'), may hold values from -6 to 6
- momentum: float32 [8192, 2, 128], P('dom'), may hold values from -6 to 6
- depth: float32 [8192, 128], P('dom'), may hold values from 0.3 to 1.5
- drag: float32 [8192, 128], P('dom'), may hold values from 0.05 to 0.6
- div_weight: float32 [5, 2, 128, 128], replicated, may hold values from -0.078125 to 0.078125
- grad_weight: float32 [5, 128, 256], replicated, may hold values from -0.125 to 0.125
- neighbours: int32 [8192, 4], P('dom'), may hold values from 0 to 8191, as said below
- wet: int32 [4, 8192], P(None, 'dom'), may hold values from 0 to 1, as said below
- boundary_cells: int32 [8192], P('dom'), may hold values from 0 to 32767, as said below
- boundary_source: int32 [8192], P('dom'), may hold values from 0 to 4095
- series: float32 [4, 4096], P(None, 'dom'), may hold values from -6 to 6
- moved_from: int32 [8192], P('dom'), may hold values from 0 to 8191, as said below
Outputs:
- level_out: float32 [8192, 128], P('dom')
- flow_out: float32 [8192, 2, 128], P('dom')
Inputs may be any that keep to these rules, and one draw needn't show every extreme that they name: Slots are left, right, lower, upper; the relation is mutual (b is c's right iff c is b's left, likewise lower and upper). Left and right neighbours lie on the block's own device; a lower neighbour lies on the block's own device or on the device of index one lower, an upper one on its own device or on the device of index one higher (wrapping around). No block has neighbours on both adjacent devices. Exactly 128 blocks of a device have a neighbour on the lower adjacent device, and exactly 128 on the upper one. 1 marks a block that is wet in that step. `boundary_cells`: block times 128 plus element, within the device that holds the entry; distinct within a device. `moved_from`: A permutation. The blocks that move from one device to one device (itself included) number at most 16, and some pair reaches that in every draw.
All inputs are finite; a program needn't handle non-finite values.
Results may differ from a plain program's by a relative error of at most 0.0001.
Values sent between devices are 32-bit elements; how exact they have to be, the bound alone decides.
A program may use at most 64 MiB of HBM per device.

v0:
```python
import functools

import jax
import jax.numpy as jnp
from jax import lax
from jax.experimental import pallas as pl
from jax.experimental.pallas import tpu as pltpu
from jax.sharding import PartitionSpec as P

MESH = pl.DeviceIdType.MESH
f32 = jnp.float32
bf16 = jnp.bfloat16
relax_rate = 0.5


def halves(x):
    hi = x.astype(bf16)
    return hi, (x - hi.astype(f32)).astype(bf16)


def mm(a, b):
    return jnp.dot(a, b, preferred_element_type=f32)


def mm3(hi, lo, w_hi, w_lo):
    return mm(hi, w_hi) + (mm(lo, w_hi) + mm(hi, w_lo))


def hot(cond):
    return jnp.where(cond, 1.0, 0.0).astype(f32)


def iota(shape, dim):
    return lax.broadcasted_iota(jnp.int32, shape, dim).astype(f32)


def kernel(
    n, slots,
    elev_ref, mom_ref, depth_ref, drag_ref, divw_ref, gradw_ref, nb_ref, wet_ref,
    cells_ref, source_ref, series_ref, moved_ref,
    level_out, flow_out,
    meta, gathered, x_ref, dw_hi, dw_lo, gw_hi, gw_lo, damp_ref, depth_p, near_ref,
    force_ref, relax_ref, div_send, div_recv, lev_send, lev_recv, pack, packed, landed,
    meta_ss, meta_rs, div_ss, div_rs, lev_ss, lev_rs, mig_ss, mig_rs,
):
    me = lax.axis_index("dom")
    up = lax.rem(me + 1, n)
    down = lax.rem(me + n - 1, n)
    steps, width = series_ref.shape
    blocks, cells = elev_ref.shape
    half = blocks // 2
    span = blocks // width

    barrier = pltpu.get_barrier_semaphore()

    def greet(i, _):
        pl.semaphore_signal(
            barrier, inc=1, device_id=(lax.rem(me + i, n),), device_id_type=MESH
        )
        return 0

    lax.fori_loop(1, n, greet, 0)

    moved = moved_ref[...].astype(f32)
    meta[...] = jnp.zeros_like(meta)
    meta[0:steps, :] = series_ref[...]
    for i in range(span):
        meta[steps + i : steps + i + 1, :] = moved[:, i * width : (i + 1) * width]
    gathered[pl.ds(me, 1)] = meta[...][None]

    pl.semaphore_wait(barrier, n - 1)

    def tile_copy(target, source):
        return pltpu.make_async_remote_copy(
            src_ref=meta,
            dst_ref=gathered.at[source],
            send_sem=meta_ss.at[target],
            recv_sem=meta_rs.at[source],
            device_id=(target,),
            device_id_type=MESH,
        )

    def send_tile(i, _):
        tile_copy(lax.rem(me + i, n), me).start()
        return 0

    lax.fori_loop(1, n, send_tile, 0)

    base = (me * blocks).astype(f32)
    square = (blocks, blocks)
    sub, lane = iota(square, 0), iota(square, 1)
    nb = nb_ref[...].astype(f32)
    nbl = nb - base
    lower_own = jnp.logical_and(nbl[2:3] >= 0.0, nbl[2:3] < float(blocks))
    key_row = jnp.where(lower_own, nb[3:4] + float(blocks), lane[0:1])
    key_col = jnp.sum(jnp.where(sub == lane, key_row, 0.0), axis=1, keepdims=True)
    pos_row = jnp.sum(hot(key_col < key_row), axis=0, keepdims=True)
    pos_col = jnp.sum(hot(key_row < key_col), axis=1, keepdims=True)
    order = hot(sub == pos_row)
    order16 = order.astype(bf16)

    def place(ids):
        return jnp.sum(jnp.where(sub[:, : ids.shape[1]] == ids, pos_col, 0.0), axis=0, keepdims=True)

    vertical = jnp.where(lower_own, nbl[2:3], nbl[3:4])
    for k, ids in enumerate((nbl[0:1], nbl[1:2], vertical)):
        col = jnp.sum(order * place(ids), axis=1, keepdims=True)
        near_ref[k * blocks : (k + 1) * blocks, :] = hot(lane == col).astype(bf16)

    field = jnp.concatenate(
        [
            mom_ref[pl.ds(0, blocks, 2), :],
            mom_ref[pl.ds(1, blocks, 2), :],
            elev_ref[...],
            depth_ref[...],
            drag_ref[...],
        ],
        axis=1,
    )
    hi, lo = halves(field)
    field = mm(order16, hi) + mm(order16, lo)
    x_ref[...] = field[:, : 2 * cells]
    elevation0 = field[:, 2 * cells : 3 * cells]
    depth_p[...] = field[:, 3 * cells : 4 * cells]
    damping = 1.0 / (1.0 + field[:, 4 * cells :])
    wet = wet_ref[...].astype(f32)
    for s in range(steps):
        mask = jnp.sum(order * wet[s : s + 1], axis=1, keepdims=True)
        damp_ref[s, :, :cells] = jnp.broadcast_to(mask, (blocks, cells))
        damp_ref[s, :, cells:] = mask * damping
    hi, lo = halves(divw_ref[...])
    dw_hi[...] = hi
    dw_lo[...] = lo
    hi, lo = halves(gradw_ref[...])
    gw_hi[...] = hi
    gw_lo[...] = lo

    def tile_done(i, _):
        source = lax.rem(me + i, n)
        tile_copy(source, source).wait_recv()
        return 0

    lax.fori_loop(1, n, tile_done, 0)
    tall = meta.shape[0]
    entries = cells_ref.shape[1]
    point = source_ref[...].astype(f32)
    chunk = jnp.floor((point + 0.5) * (1.0 / width))
    spot = point - chunk * width
    pick = hot(iota((width, entries), 0) == spot).astype(bf16)
    everyone = gathered[...]
    hi, lo = halves(everyone.reshape(n * tall, width))
    found = (mm(hi, pick) + mm(lo, pick)).reshape(n, tall, entries)
    found = jnp.sum(jnp.where(iota(found.shape, 0) == chunk[None], found, 0.0), axis=0)
    cell = cells_ref[...].astype(f32)
    block = jnp.floor((cell + 0.5) * (1.0 / cells))
    element = cell - block * cells
    block_place = jnp.sum(
        jnp.where(iota((blocks, entries), 0) == block, pos_col, 0.0), axis=0, keepdims=True
    )
    rows = hot(iota((blocks, entries), 0) == block_place).astype(bf16)
    columns = hot(iota((cells, entries), 0) == element)

    def spread(values):
        return lax.dot_general(
            rows, values, (((1,), (1,)), ((), ())), preferred_element_type=f32
        )

    relax_ref[...] = relax_rate * spread(columns.astype(bf16))
    for s in range(steps):
        hi, lo = halves(columns * found[s : s + 1])
        force_ref[s] = spread(hi) + spread(lo)

    takes = jnp.concatenate([everyone[:, steps + i, :] for i in range(span)], axis=1) - base
    mine = hot(jnp.logical_and(takes >= 0.0, takes < float(blocks)))
    rank = mm(mine.astype(bf16), hot(sub < lane).astype(bf16))
    rank = jnp.where(mine > 0.0, rank, -1.0)
    cube = (n, slots, blocks)
    chosen = jnp.where(rank[:, None, :] == iota(cube, 1), takes[:, None, :] + 1.0, 0.0)
    chosen = jnp.sum(chosen.reshape(n * slots, blocks), axis=1, keepdims=True) - 1.0
    lanes = iota((n * slots, blocks), 1)
    pack[...] = mm(hot(lanes == chosen).astype(bf16), hot(lane == pos_col).astype(bf16)).astype(bf16)

    def halo(send, recv, ss, rs, step, way):
        return pltpu.make_async_remote_copy(
            src_ref=send,
            dst_ref=recv.at[step, way],
            send_sem=ss.at[step, way],
            recv_sem=rs.at[step, way],
            device_id=((up, down)[way],),
            device_id_type=MESH,
        )

    def div_copy(step, way):
        return halo(div_send.at[step, way], div_recv, div_ss, div_rs, step, way)

    def lev_copy(step, way):
        rows_out = (pl.ds(half, half), pl.ds(0, half))[way]
        return halo(lev_send.at[step, rows_out], lev_recv, lev_ss, lev_rs, step, way)

    def sl(k, size):
        return slice(k * size, (k + 1) * size)

    wide = 2 * cells

    def one_step(step, elevation):
        x = x_ref[...]
        hi, lo = halves(x)
        for way, rows_out, slot in ((0, slice(half, blocks), 3), (1, slice(0, half), 4)):
            div_send[step, way] = mm3(
                hi[rows_out], lo[rows_out], dw_hi[sl(slot, wide), :], dw_lo[sl(slot, wide), :]
            )
            div_copy(step, way).start()
        near = mm(near_ref[...], jnp.concatenate([hi, lo], axis=1)).astype(bf16)
        three = slice(0, 3 * wide)
        hi3 = jnp.concatenate([hi, near[:blocks, :wide], near[blocks : 2 * blocks, :wide]], axis=1)
        lo3 = jnp.concatenate([lo, near[:blocks, wide:], near[blocks : 2 * blocks, wide:]], axis=1)
        div = mm3(hi3, lo3, dw_hi[three, :], dw_lo[three, :])
        upper = near[2 * blocks :]
        div = div + jnp.concatenate(
            [
                mm3(
                    upper[r, :wide], upper[r, wide:], dw_hi[sl(k, wide), :], dw_lo[sl(k, wide), :]
                )
                for r, k in ((slice(0, half), 4), (slice(half, blocks), 3))
            ],
            axis=0,
        )
        div_copy(step, 0).wait_recv()
        div_copy(step, 1).wait_recv()
        div = div + jnp.concatenate([div_recv[step, 0], div_recv[step, 1]], axis=0)
        level = elevation - damp_ref[step, :, :cells] * div
        level = level + relax_ref[...] * (force_ref[step] - level)
        lev_send[step] = level
        lev_copy(step, 0).start()
        lev_copy(step, 1).start()
        hi, lo = halves(level)
        near = mm(near_ref[...], jnp.concatenate([hi, lo], axis=1)).astype(bf16)
        three = slice(0, 3 * cells)
        hi3 = jnp.concatenate([hi, near[:blocks, :cells], near[blocks : 2 * blocks, :cells]], axis=1)
        lo3 = jnp.concatenate([lo, near[:blocks, cells:], near[blocks : 2 * blocks, cells:]], axis=1)
        grad = mm3(hi3, lo3, gw_hi[three, :], gw_lo[three, :])
        upper = near[2 * blocks :]
        grad = grad + jnp.concatenate(
            [
                mm3(
                    upper[r, :cells], upper[r, cells:],
                    gw_hi[sl(k, cells), :], gw_lo[sl(k, cells), :],
                )
                for r, k in ((slice(0, half), 4), (slice(half, blocks), 3))
            ],
            axis=0,
        )
        lev_copy(step, 0).wait_recv()
        lev_copy(step, 1).wait_recv()
        away = [
            mm3(*halves(lev_recv[step, way]), gw_hi[sl(k, cells), :], gw_lo[sl(k, cells), :])
            for way, k in ((0, 3), (1, 4))
        ]
        grad = grad + jnp.concatenate(away, axis=0)
        depth = depth_p[...]
        damp = damp_ref[step, :, cells:]
        x_ref[:, :cells] = damp * (x[:, :cells] - depth * grad[:, :cells])
        x_ref[:, cells:] = damp * (x[:, cells:] - depth * grad[:, cells:])
        return level

    level = lax.fori_loop(0, steps, one_step, elevation0)

    state = jnp.concatenate([level, x_ref[...]], axis=1)
    hi, lo = halves(state)
    moving = mm(pack[...], hi) + mm(pack[...], lo)
    packed[...] = moving.reshape(packed.shape)
    landed[pl.ds(me, 1)] = packed[pl.ds(me, 1)]

    def state_copy(target, source):
        return pltpu.make_async_remote_copy(
            src_ref=packed.at[target],
            dst_ref=landed.at[source],
            send_sem=mig_ss.at[target],
            recv_sem=mig_rs.at[source],
            device_id=(target,),
            device_id_type=MESH,
        )

    def send_state(i, _):
        state_copy(lax.rem(me + i, n), me).start()
        return 0

    lax.fori_loop(1, n, send_state, 0)

    owner_row = jnp.floor((moved + 0.5) * (1.0 / blocks))
    owner_col = jnp.sum(jnp.where(sub == lane, owner_row, 0.0), axis=1, keepdims=True)
    ahead = jnp.sum(
        jnp.where(lane < sub, hot(owner_row == owner_col), 0.0), axis=1, keepdims=True
    )
    where_from = owner_col * float(slots) + ahead
    unpack = hot(iota((blocks, n * slots), 1) == where_from).astype(bf16)

    def state_done(i, _):
        source = lax.rem(me + i, n)
        state_copy(source, source).wait_recv()
        return 0

    lax.fori_loop(1, n, state_done, 0)
    hi, lo = halves(landed[...].reshape(n * slots, 3 * cells))
    result = mm(unpack, hi) + mm(unpack, lo)
    level_out[...] = result[:, :cells]
    flow_out[pl.ds(0, blocks, 2), :] = result[:, cells : 2 * cells]
    flow_out[pl.ds(1, blocks, 2), :] = result[:, 2 * cells :]

    def sent(i, _):
        target = lax.rem(me + i, n)
        tile_copy(target, me).wait_send()
        state_copy(target, me).wait_send()
        return 0

    lax.fori_loop(1, n, sent, 0)

    def halo_sent(step, _):
        for way in (0, 1):
            div_copy(step, way).wait_send()
            lev_copy(step, way).wait_send()
        return 0

    lax.fori_loop(0, steps, halo_sent, 0)


def local(
    n,
    elevation,
    momentum,
    depth,
    drag,
    div_weight,
    grad_weight,
    neighbours,
    wet,
    boundary_cells,
    boundary_source,
    series,
    moved_from,
):
    blocks, cells = elevation.shape
    steps, width = series.shape
    half = blocks // 2
    wide = 2 * cells
    portion = 2 * blocks // n
    slots = -(-portion // 8) * 8
    tall = -(-(steps + blocks // width) // 8) * 8
    vmem, dma = pltpu.VMEM, pltpu.SemaphoreType.DMA
    level, flow = pl.pallas_call(
        functools.partial(kernel, n, slots),
        out_shape=(
            jax.ShapeDtypeStruct((blocks, cells), f32),
            jax.ShapeDtypeStruct((2 * blocks, cells), f32),
        ),
        in_specs=[pl.BlockSpec(memory_space=vmem)] * 12,
        out_specs=(pl.BlockSpec(memory_space=vmem),) * 2,
        scratch_shapes=[
            vmem((tall, width), f32),
            vmem((n, tall, width), f32),
            vmem((blocks, wide), f32),
            vmem((5 * wide, cells), bf16),
            vmem((5 * wide, cells), bf16),
            vmem((5 * cells, wide), bf16),
            vmem((5 * cells, wide), bf16),
            vmem((steps, blocks, wide), f32),
            vmem((blocks, cells), f32),
            vmem((3 * blocks, blocks), bf16),
            vmem((steps, blocks, cells), f32),
            vmem((blocks, cells), f32),
            vmem((steps, 2, half, cells), f32),
            vmem((steps, 2, half, cells), f32),
            vmem((steps, blocks, cells), f32),
            vmem((steps, 2, half, cells), f32),
            vmem((n * slots, blocks), bf16),
            vmem((n, slots, 3 * cells), f32),
            vmem((n, slots, 3 * cells), f32),
            dma((n,)),
            dma((n,)),
            dma((steps, 2)),
            dma((steps, 2)),
            dma((steps, 2)),
            dma((steps, 2)),
            dma((n,)),
            dma((n,)),
        ],
        compiler_params=pltpu.CompilerParams(
            collective_id=0, has_side_effects=True, vmem_limit_bytes=48 * 1024 * 1024
        ),
        name="surge",
    )(
        elevation,
        momentum.reshape(2 * blocks, cells),
        depth,
        drag,
        div_weight.reshape(5 * wide, cells),
        grad_weight.reshape(5 * cells, wide),
        neighbours.T,
        wet,
        boundary_cells.reshape(1, -1),
        boundary_source.reshape(1, -1),
        series,
        moved_from.reshape(1, -1),
    )
    return level, flow.reshape(blocks, 2, cells)


def solution(mesh):
    n = mesh.shape["dom"]
    return jax.shard_map(
        functools.partial(local, n),
        mesh=mesh,
        in_specs=(
            P("dom", None),
            P("dom", None, None),
            P("dom", None),
            P("dom", None),
            P(),
            P(),
            P("dom", None),
            P(None, "dom"),
            P("dom"),
            P("dom"),
            P(None, "dom"),
            P("dom"),
        ),
        out_specs=(P("dom", None), P("dom", None, None)),
        check_vma=False,
    )
```

profile of v0, /device:TPU:0, one launch (start us, length us, event | category | flops | bytes accessed | tf_op | source)
XLA Modules:
  0.0 74.4 jit_solution(676454127355275981)
XLA Ops:
  0.6 0.0 copy-start.10
  0.6 0.0 copy-start.11
  0.7 0.0 copy-start.8
  0.7 0.0 copy-start.7
  0.7 0.0 copy-start.6
  0.7 0.0 copy-start.9
  0.7 0.6 copy-done.10
  1.3 0.0 copy-done.11
  1.3 0.0 copy-done.8
  1.3 0.0 copy-done.7
  1.4 0.0 copy-done.6
  1.4 0.0 copy-done.9
  1.4 0.0 copy-start
  1.4 1.1 %copy-done = f32[5,2,128,128]{3,2,1,0:T(8,128)S(1)} copy-done((f32[5,2,128,128]{3,2,1,0:T(8,128)S(1)}, f32[5,2,128,128]{3,2,1,0:T(8,128)}, u32[]{:S(2)}) %copy-start) | copy-done | bytes 655384
  2.5 0.0 copy-start.1
  2.5 1.1 %copy-done.1 = f32[5,128,256]{2,1,0:T(8,128)S(1)} copy-done((f32[5,128,256]{2,1,0:T(8,128)S(1)}, f32[5,128,256]{2,1,0:T(8,128)}, u32[]{:S(2)}) %copy-start.1) | copy-done | bytes 655384
  3.6 0.0 copy-start.2
  3.6 0.9 %copy-done.2 = f32[256,2,128]{2,1,0:T(2,128)S(1)} copy-done((f32[256,2,128]{2,1,0:T(2,128)S(1)}, f32[256,2,128]{2,1,0:T(2,128)}, u32[]{:S(2)}) %copy-start.2) | copy-done | bytes 262168
  4.5 0.0 copy-start.3
  4.5 0.9 %copy-done.3 = f32[256,128]{1,0:T(8,128)S(1)} copy-done((f32[256,128]{1,0:T(8,128)S(1)}, f32[256,128]{1,0:T(8,128)}, u32[]{:S(2)}) %copy-start.3) | copy-done | bytes 131096
  5.4 0.0 copy-start.4
  5.4 0.9 %copy-done.4 = f32[256,128]{1,0:T(8,128)S(1)} copy-done((f32[256,128]{1,0:T(8,128)S(1)}, f32[256,128]{1,0:T(8,128)}, u32[]{:S(2)}) %copy-start.4) | copy-done | bytes 131096
  6.3 0.0 copy-start.5
  6.3 0.9 %copy-done.5 = f32[256,128]{1,0:T(8,128)S(1)} copy-done((f32[256,128]{1,0:T(8,128)S(1)}, f32[256,128]{1,0:T(8,128)}, u32[]{:S(2)}) %copy-start.5) | copy-done | bytes 131096
  7.2 65.8 %surge.1 = (f32[256,128]{1,0:T(8,128)S(1)}, f32[512,128]{1,0:T(8,128)S(1)}) custom-call(f32[256,128]{1,0:T(8,128)S(1)} %copy-done.3, f32[512,128]{1,0:T(8,128)S(1)} %bitcast.10, f32[256,128]{1,0:T(8,128)S(1)} %copy-done.4, f32[256,128]{1,0:T(8,128)S(1)} %copy-done.5, f32[1280,128]{1,0:T(8,128)S(1)} %bitcast.8, f32[640,256]{1,0:T(8,128)S(1)} %bitcast.9, ...), custom_call_target="tpu_custom_call" | custom-call | tf_op jit(solution)/shard_map/surge/pallas_call | solution.py:350
  73.1 0.7 copy.16
  73.7 0.7 copy.17
Async XLA Ops:
  0.6 0.7 copy-start.10
  0.6 0.7 copy-start.11
  0.7 0.7 copy-start.8
  0.7 0.7 copy-start.7
  0.7 0.7 copy-start.6
  0.7 0.7 copy-start.9
  1.4 1.1 %copy-start = (f32[5,2,128,128]{3,2,1,0:T(8,128)S(1)}, f32[5,2,128,128]{3,2,1,0:T(8,128)}, u32[]{:S(2)}) copy-start(f32[5,2,128,128]{3,2,1,0:T(8,128)} %param.16) | copy-start | bytes 1966084
  2.5 1.1 %copy-start.1 = (f32[5,128,256]{2,1,0:T(8,128)S(1)}, f32[5,128,256]{2,1,0:T(8,128)}, u32[]{:S(2)}) copy-start(f32[5,128,256]{2,1,0:T(8,128)} %param.17) | copy-start | bytes 1966084
  3.6 0.9 %copy-start.2 = (f32[256,2,128]{2,1,0:T(2,128)S(1)}, f32[256,2,128]{2,1,0:T(2,128)}, u32[]{:S(2)}) copy-start(f32[256,2,128]{2,1,0:T(2,128)} %param.13) | copy-start | bytes 786436
  4.5 0.9 %copy-start.3 = (f32[256,128]{1,0:T(8,128)S(1)}, f32[256,128]{1,0:T(8,128)}, u32[]{:S(2)}) copy-start(f32[256,128]{1,0:T(8,128)} %elev_ref.1) | copy-start | bytes 393220
  5.4 0.9 %copy-start.4 = (f32[256,128]{1,0:T(8,128)S(1)}, f32[256,128]{1,0:T(8,128)}, u32[]{:S(2)}) copy-start(f32[256,128]{1,0:T(8,128)} %depth_ref.1) | copy-start | bytes 393220
  6.3 0.9 %copy-start.5 = (f32[256,128]{1,0:T(8,128)S(1)}, f32[256,128]{1,0:T(8,128)}, u32[]{:S(2)}) copy-start(f32[256,128]{1,0:T(8,128)} %drag_ref.1) | copy-start | bytes 393220
where the time goes:
time: 74.9 us; the launch traced here: 74.4 us
  Pallas kernels  65.8 us (88%)
  local copies, waits for them, and re-layouts  7.9 us (11%)
    pallas_call x1, Pallas kernels, local(): pl.pallas_call(functools.partial(kernel, n, slots), out_shape=(jax.ShapeD...  65.8 us
    unnamed x26, local copies, waits for them, and re-layouts  7.9 us

commit v1 on v0

--- a/solution.py
+++ b/solution.py
@@ -36,12 +36,14 @@
 
 def kernel(
     n, slots,
+    elev_hbm, mom_hbm, depth_hbm, drag_hbm, divw_hbm, gradw_hbm, nb_hbm, wet_hbm,
+    cells_hbm, source_hbm, series_hbm, moved_hbm,
+    level_out, flow_out,
     elev_ref, mom_ref, depth_ref, drag_ref, divw_ref, gradw_ref, nb_ref, wet_ref,
     cells_ref, source_ref, series_ref, moved_ref,
-    level_out, flow_out,
     meta, gathered, x_ref, dw_hi, dw_lo, gw_hi, gw_lo, damp_ref, depth_p, near_ref,
     force_ref, relax_ref, div_send, div_recv, lev_send, lev_recv, pack, packed, landed,
-    meta_ss, meta_rs, div_ss, div_rs, lev_ss, lev_rs, mig_ss, mig_rs,
+    in_ss, meta_ss, meta_rs, div_ss, div_rs, lev_ss, lev_rs, mig_ss, mig_rs,
 ):
     me = lax.axis_index("dom")
     up = lax.rem(me + 1, n)
@@ -49,7 +51,30 @@
     steps, width = series_ref.shape
     blocks, cells = elev_ref.shape
     half = blocks // 2
+    wide = 2 * cells
     span = blocks // width
+
+    inputs = [
+        pltpu.make_async_copy(src, dst, in_ss.at[i])
+        for i, (src, dst) in enumerate(
+            (
+                (nb_hbm, nb_ref),
+                (moved_hbm, moved_ref),
+                (series_hbm, series_ref),
+                (wet_hbm, wet_ref),
+                (cells_hbm, cells_ref),
+                (source_hbm, source_ref),
+                (mom_hbm, mom_ref),
+                (elev_hbm, elev_ref),
+                (depth_hbm, depth_ref),
+                (drag_hbm, drag_ref),
+                (divw_hbm, divw_ref),
+                (gradw_hbm, gradw_ref),
+            )
+        )
+    ]
+    for copy in inputs:
+        copy.start()
 
     barrier = pltpu.get_barrier_semaphore()
 
@@ -61,31 +86,15 @@
 
     lax.fori_loop(1, n, greet, 0)
 
-    moved = moved_ref[...].astype(f32)
-    meta[...] = jnp.zeros_like(meta)
-    meta[0:steps, :] = series_ref[...]
-    for i in range(span):
-        meta[steps + i : steps + i + 1, :] = moved[:, i * width : (i + 1) * width]
-    gathered[pl.ds(me, 1)] = meta[...][None]
-
-    pl.semaphore_wait(barrier, n - 1)
-
-    def tile_copy(target, source):
-        return pltpu.make_async_remote_copy(
-            src_ref=meta,
-            dst_ref=gathered.at[source],
-            send_sem=meta_ss.at[target],
-            recv_sem=meta_rs.at[source],
-            device_id=(target,),
-            device_id_type=MESH,
-        )
-
-    def send_tile(i, _):
-        tile_copy(lax.rem(me + i, n), me).start()
-        return 0
-
-    lax.fori_loop(1, n, send_tile, 0)
-
+    def partner(i):
+        j = i - 1
+        return lax.rem(me + (j + 1) // 2 + (1 - j % 2) * (n // 2), n)
+
+    def sl(k, size):
+        return slice(k * size, (k + 1) * size)
+
+    for copy in inputs[:6]:
+        copy.wait()
     base = (me * blocks).astype(f32)
     square = (blocks, blocks)
     sub, lane = iota(square, 0), iota(square, 1)
@@ -99,14 +108,8 @@
     order = hot(sub == pos_row)
     order16 = order.astype(bf16)
 
-    def place(ids):
-        return jnp.sum(jnp.where(sub[:, : ids.shape[1]] == ids, pos_col, 0.0), axis=0, keepdims=True)
-
-    vertical = jnp.where(lower_own, nbl[2:3], nbl[3:4])
-    for k, ids in enumerate((nbl[0:1], nbl[1:2], vertical)):
-        col = jnp.sum(order * place(ids), axis=1, keepdims=True)
-        near_ref[k * blocks : (k + 1) * blocks, :] = hot(lane == col).astype(bf16)
-
+    for copy in inputs[6:10]:
+        copy.wait()
     field = jnp.concatenate(
         [
             mom_ref[pl.ds(0, blocks, 2), :],
@@ -119,66 +122,14 @@
     )
     hi, lo = halves(field)
     field = mm(order16, hi) + mm(order16, lo)
-    x_ref[...] = field[:, : 2 * cells]
-    elevation0 = field[:, 2 * cells : 3 * cells]
+    x_ref[...] = field[:, :wide]
+    elevation0 = field[:, wide : 3 * cells]
     depth_p[...] = field[:, 3 * cells : 4 * cells]
     damping = 1.0 / (1.0 + field[:, 4 * cells :])
-    wet = wet_ref[...].astype(f32)
-    for s in range(steps):
-        mask = jnp.sum(order * wet[s : s + 1], axis=1, keepdims=True)
-        damp_ref[s, :, :cells] = jnp.broadcast_to(mask, (blocks, cells))
-        damp_ref[s, :, cells:] = mask * damping
+    inputs[10].wait()
     hi, lo = halves(divw_ref[...])
     dw_hi[...] = hi
     dw_lo[...] = lo
-    hi, lo = halves(gradw_ref[...])
-    gw_hi[...] = hi
-    gw_lo[...] = lo
-
-    def tile_done(i, _):
-        source = lax.rem(me + i, n)
-        tile_copy(source, source).wait_recv()
-        return 0
-
-    lax.fori_loop(1, n, tile_done, 0)
-    tall = meta.shape[0]
-    entries = cells_ref.shape[1]
-    point = source_ref[...].astype(f32)
-    chunk = jnp.floor((point + 0.5) * (1.0 / width))
-    spot = point - chunk * width
-    pick = hot(iota((width, entries), 0) == spot).astype(bf16)
-    everyone = gathered[...]
-    hi, lo = halves(everyone.reshape(n * tall, width))
-    found = (mm(hi, pick) + mm(lo, pick)).reshape(n, tall, entries)
-    found = jnp.sum(jnp.where(iota(found.shape, 0) == chunk[None], found, 0.0), axis=0)
-    cell = cells_ref[...].astype(f32)
-    block = jnp.floor((cell + 0.5) * (1.0 / cells))
-    element = cell - block * cells
-    block_place = jnp.sum(
-        jnp.where(iota((blocks, entries), 0) == block, pos_col, 0.0), axis=0, keepdims=True
-    )
-    rows = hot(iota((blocks, entries), 0) == block_place).astype(bf16)
-    columns = hot(iota((cells, entries), 0) == element)
-
-    def spread(values):
-        return lax.dot_general(
-            rows, values, (((1,), (1,)), ((), ())), preferred_element_type=f32
-        )
-
-    relax_ref[...] = relax_rate * spread(columns.astype(bf16))
-    for s in range(steps):
-        hi, lo = halves(columns * found[s : s + 1])
-        force_ref[s] = spread(hi) + spread(lo)
-
-    takes = jnp.concatenate([everyone[:, steps + i, :] for i in range(span)], axis=1) - base
-    mine = hot(jnp.logical_and(takes >= 0.0, takes < float(blocks)))
-    rank = mm(mine.astype(bf16), hot(sub < lane).astype(bf16))
-    rank = jnp.where(mine > 0.0, rank, -1.0)
-    cube = (n, slots, blocks)
-    chosen = jnp.where(rank[:, None, :] == iota(cube, 1), takes[:, None, :] + 1.0, 0.0)
-    chosen = jnp.sum(chosen.reshape(n * slots, blocks), axis=1, keepdims=True) - 1.0
-    lanes = iota((n * slots, blocks), 1)
-    pack[...] = mm(hot(lanes == chosen).astype(bf16), hot(lane == pos_col).astype(bf16)).astype(bf16)
 
     def halo(send, recv, ss, rs, step, way):
         return pltpu.make_async_remote_copy(
@@ -197,19 +148,120 @@
         rows_out = (pl.ds(half, half), pl.ds(0, half))[way]
         return halo(lev_send.at[step, rows_out], lev_recv, lev_ss, lev_rs, step, way)
 
-    def sl(k, size):
-        return slice(k * size, (k + 1) * size)
-
-    wide = 2 * cells
-
-    def one_step(step, elevation):
+    def tile_copy(target, source):
+        return pltpu.make_async_remote_copy(
+            src_ref=meta,
+            dst_ref=gathered.at[source],
+            send_sem=meta_ss.at[target],
+            recv_sem=meta_rs.at[source],
+            device_id=(target,),
+            device_id_type=MESH,
+        )
+
+    def state_copy(target, source):
+        return pltpu.make_async_remote_copy(
+            src_ref=packed.at[target],
+            dst_ref=landed.at[source],
+            send_sem=mig_ss.at[target],
+            recv_sem=mig_rs.at[source],
+            device_id=(target,),
+            device_id_type=MESH,
+        )
+
+    moved = moved_ref[...].astype(f32)
+
+    def open_up():
+        meta[...] = jnp.zeros_like(meta)
+        meta[0:steps, :] = series_ref[...]
+        for i in range(span):
+            meta[steps + i : steps + i + 1, :] = moved[:, i * width : (i + 1) * width]
+        gathered[pl.ds(me, 1)] = meta[...][None]
+        pl.semaphore_wait(barrier, n - 1)
+
+    def send_tiles():
+        def send(i, _):
+            tile_copy(partner(i), me).start()
+            return 0
+
+        lax.fori_loop(1, n, send, 0)
+
+        def place(ids):
+            return jnp.sum(jnp.where(sub == ids, pos_col, 0.0), axis=0, keepdims=True)
+
+        vertical = jnp.where(lower_own, nbl[2:3], nbl[3:4])
+        for k, ids in enumerate((nbl[0:1], nbl[1:2], vertical)):
+            col = jnp.sum(order * place(ids), axis=1, keepdims=True)
+            near_ref[sl(k, blocks), :] = hot(lane == col).astype(bf16)
+        wet = wet_ref[...].astype(f32)
+        for s in range(steps):
+            mask = jnp.sum(order * wet[s : s + 1], axis=1, keepdims=True)
+            damp_ref[s, :, :cells] = jnp.broadcast_to(mask, (blocks, cells))
+            damp_ref[s, :, cells:] = mask * damping
+
+    def boundary():
+        entries = cells_ref.shape[1]
+        point = source_ref[...].astype(f32)
+        chunk = jnp.floor((point + 0.5) * (1.0 / width))
+        spot = point - chunk * width
+        pick = hot(iota((width, entries), 0) == spot).astype(bf16)
+        cell = cells_ref[...].astype(f32)
+        block = jnp.floor((cell + 0.5) * (1.0 / cells))
+        element = cell - block * cells
+        block_place = jnp.sum(
+            jnp.where(iota((blocks, entries), 0) == block, pos_col, 0.0), axis=0, keepdims=True
+        )
+        rows = hot(iota((blocks, entries), 0) == block_place).astype(bf16)
+        columns = hot(iota((cells, entries), 0) == element)
+
+        def spread(values):
+            return lax.dot_general(
+                rows, values, (((1,), (1,)), ((), ())), preferred_element_type=f32
+            )
+
+        relax_ref[...] = relax_rate * spread(columns.astype(bf16))
+
+        def tile_done(i, _):
+            source = lax.rem(me + i, n)
+            tile_copy(source, source).wait_recv()
+            return 0
+
+        lax.fori_loop(1, n, tile_done, 0)
+        tall = meta.shape[0]
+        hi, lo = halves(gathered[...].reshape(n * tall, width))
+        found = (mm(hi, pick) + mm(lo, pick)).reshape(n, tall, entries)
+        found = jnp.sum(jnp.where(iota(found.shape, 0) == chunk[None], found, 0.0), axis=0)
+        for s in range(steps):
+            hi, lo = halves(columns * found[s : s + 1])
+            force_ref[s] = spread(hi) + spread(lo)
+
+    def choose():
+        everyone = gathered[...]
+        takes = jnp.concatenate([everyone[:, steps + i, :] for i in range(span)], axis=1) - base
+        mine = hot(jnp.logical_and(takes >= 0.0, takes < float(blocks)))
+        rank = mm(mine.astype(bf16), hot(sub < lane).astype(bf16))
+        rank = jnp.where(mine > 0.0, rank, -1.0)
+        cube = (n, slots, blocks)
+        chosen = jnp.where(rank[:, None, :] == iota(cube, 1), takes[:, None, :] + 1.0, 0.0)
+        chosen = jnp.sum(chosen.reshape(n * slots, blocks), axis=1, keepdims=True) - 1.0
+        lanes = iota((n * slots, blocks), 1)
+        pack[...] = mm(
+            hot(lanes == chosen).astype(bf16), hot(lane == pos_col).astype(bf16)
+        ).astype(bf16)
+
+    def one_step(step, elevation, opening):
         x = x_ref[...]
         hi, lo = halves(x)
         for way, rows_out, slot in ((0, slice(half, blocks), 3), (1, slice(0, half), 4)):
             div_send[step, way] = mm3(
                 hi[rows_out], lo[rows_out], dw_hi[sl(slot, wide), :], dw_lo[sl(slot, wide), :]
             )
-            div_copy(step, way).start()
+            if not opening:
+                div_copy(step, way).start()
+        if opening:
+            open_up()
+            for way in (0, 1):
+                div_copy(step, way).start()
+            send_tiles()
         near = mm(near_ref[...], jnp.concatenate([hi, lo], axis=1)).astype(bf16)
         three = slice(0, 3 * wide)
         hi3 = jnp.concatenate([hi, near[:blocks, :wide], near[blocks : 2 * blocks, :wide]], axis=1)
@@ -225,6 +277,8 @@
             ],
             axis=0,
         )
+        if opening:
+            boundary()
         div_copy(step, 0).wait_recv()
         div_copy(step, 1).wait_recv()
         div = div + jnp.concatenate([div_recv[step, 0], div_recv[step, 1]], axis=0)
@@ -233,6 +287,11 @@
         lev_send[step] = level
         lev_copy(step, 0).start()
         lev_copy(step, 1).start()
+        if opening:
+            inputs[11].wait()
+            hi, lo = halves(gradw_ref[...])
+            gw_hi[...] = hi
+            gw_lo[...] = lo
         hi, lo = halves(level)
         near = mm(near_ref[...], jnp.concatenate([hi, lo], axis=1)).astype(bf16)
         three = slice(0, 3 * cells)
@@ -250,6 +309,8 @@
             ],
             axis=0,
         )
+        if opening:
+            choose()
         lev_copy(step, 0).wait_recv()
         lev_copy(step, 1).wait_recv()
         away = [
@@ -263,7 +324,8 @@
         x_ref[:, cells:] = damp * (x[:, cells:] - depth * grad[:, cells:])
         return level
 
-    level = lax.fori_loop(0, steps, one_step, elevation0)
+    level = one_step(0, elevation0, True)
+    level = lax.fori_loop(1, steps, lambda s, e: one_step(s, e, False), level)
 
     state = jnp.concatenate([level, x_ref[...]], axis=1)
     hi, lo = halves(state)
@@ -271,18 +333,8 @@
     packed[...] = moving.reshape(packed.shape)
     landed[pl.ds(me, 1)] = packed[pl.ds(me, 1)]
 
-    def state_copy(target, source):
-        return pltpu.make_async_remote_copy(
-            src_ref=packed.at[target],
-            dst_ref=landed.at[source],
-            send_sem=mig_ss.at[target],
-            recv_sem=mig_rs.at[source],
-            device_id=(target,),
-            device_id_type=MESH,
-        )
-
     def send_state(i, _):
-        state_copy(lax.rem(me + i, n), me).start()
+        state_copy(partner(i), me).start()
         return 0
 
     lax.fori_loop(1, n, send_state, 0)
@@ -353,9 +405,21 @@
             jax.ShapeDtypeStruct((blocks, cells), f32),
             jax.ShapeDtypeStruct((2 * blocks, cells), f32),
         ),
-        in_specs=[pl.BlockSpec(memory_space=vmem)] * 12,
+        in_specs=[pl.BlockSpec(memory_space=pl.ANY)] * 12,
         out_specs=(pl.BlockSpec(memory_space=vmem),) * 2,
         scratch_shapes=[
+            vmem((blocks, cells), f32),
+            vmem((2 * blocks, cells), f32),
+            vmem((blocks, cells), f32),
+            vmem((blocks, cells), f32),
+            vmem((5 * wide, cells), f32),
+            vmem((5 * cells, wide), f32),
+            vmem((4, blocks), jnp.int32),
+            vmem(wet.shape, jnp.int32),
+            vmem((1, boundary_cells.shape[0]), jnp.int32),
+            vmem((1, boundary_source.shape[0]), jnp.int32),
+            vmem(series.shape, f32),
+            vmem((1, blocks), jnp.int32),
             vmem((tall, width), f32),
             vmem((n, tall, width), f32),
             vmem((blocks, wide), f32),
@@ -375,6 +439,7 @@
             vmem((n * slots, blocks), bf16),
             vmem((n, slots, 3 * cells), f32),
             vmem((n, slots, 3 * cells), f32),
+            dma((12,)),
             dma((n,)),
             dma((n,)),
             dma((steps, 2)),
@@ -385,7 +450,7 @@
             dma((n,)),
         ],
         compiler_params=pltpu.CompilerParams(
-            collective_id=0, has_side_effects=True, vmem_limit_bytes=48 * 1024 * 1024
+            collective_id=0, has_side_effects=True, vmem_limit_bytes=60 * 1024 * 1024
         ),
         name="surge",
     )(

time: 74.9 us -> 66 us (0.88)
  local copies, waits for them, and re-layouts: 7.9 us -> 2.32 us
  Pallas kernels: 65.8 us -> 62.5 us
    unnamed x26 -> x4, local copies, waits for them, and re-layouts: 7.9 us -> 2.32 us
    pallas_call x1, Pallas kernels: 65.8 us -> 62.5 us  [local(): pl.pallas_call(functools.partial(kernel, n, slots), out_shape=(jax.ShapeD...]
where the time goes in v1:
time: 66 us; the launch traced here: 65.4 us
  Pallas kernels  62.5 us (95%)
  local copies, waits for them, and re-layouts  2.32 us (4%)
    pallas_call x1, Pallas kernels, local(): pl.pallas_call(functools.partial(kernel, n, slots), out_shape=(jax.ShapeD...  62.5 us
    unnamed x4, local copies, waits for them, and re-layouts  2.32 us

profile of v1, /device:TPU:0, one launch (start us, length us, event | category | flops | bytes accessed | tf_op | source)
XLA Modules:
  0.0 65.4 jit_solution(3261432585027339548)
XLA Ops:
  0.6 62.5 %surge.1 = (f32[256,128]{1,0:T(8,128)}, f32[512,128]{1,0:T(8,128)}) custom-call(f32[256,128]{1,0:T(8,128)} %elev_hbm.1, f32[512,128]{1,0:T(8,128)} %bitcast.10, f32[256,128]{1,0:T(8,128)} %depth_hbm.1, f32[256,128]{1,0:T(8,128)} %drag_hbm.1, f32[1280,128]{1,0:T(8,128)} %bitcast.8, f32[640,256]{1,0:T(8,128)} %bitcast.9, s32[4,256]{1,0:T(4,128)} %bitcast.12, ...), custom_call_target="tpu_custom_call" | custom-call | tf_op jit(solution)/shard_map/surge/pallas_call | solution.py:402
  63.1 0.0 copy-start
  63.1 1.6 %copy.16 = f32[256,128]{1,0:T(8,128)} copy(f32[256,128]{1,0:T(8,128)} %get-tuple-element.8) | data formatting | bytes 262144
  64.7 0.0 copy-done
  64.7 0.7 %copy.17 = f32[256,2,128]{2,1,0:T(2,128)} copy(f32[256,2,128]{2,1,0:T(2,128)S(1)} %bitcast.11) | data formatting | bytes 524288
Async XLA Ops:
  63.1 1.6 %copy-start = (f32[512,128]{1,0:T(8,128)S(1)}, f32[512,128]{1,0:T(8,128)}, u32[]{:S(2)}) copy-start(f32[512,128]{1,0:T(8,128)} %get-tuple-element.5) | copy-start | bytes 786436

commit v2 on v1

--- a/solution.py
+++ b/solution.py
@@ -38,12 +38,12 @@
     n, slots,
     elev_hbm, mom_hbm, depth_hbm, drag_hbm, divw_hbm, gradw_hbm, nb_hbm, wet_hbm,
     cells_hbm, source_hbm, series_hbm, moved_hbm,
-    level_out, flow_out,
+    landed_level, landed_flow,
     elev_ref, mom_ref, depth_ref, drag_ref, divw_ref, gradw_ref, nb_ref, wet_ref,
     cells_ref, source_ref, series_ref, moved_ref,
     meta, gathered, x_ref, dw_hi, dw_lo, gw_hi, gw_lo, damp_ref, depth_p, near_ref,
-    force_ref, relax_ref, div_send, div_recv, lev_send, lev_recv, pack, packed, landed,
-    in_ss, meta_ss, meta_rs, div_ss, div_rs, lev_ss, lev_rs, mig_ss, mig_rs,
+    force_ref, relax_ref, div_send, div_recv, lev_send, lev_recv, pack, packed_level, packed_flow,
+    in_ss, meta_ss, meta_rs, div_ss, div_rs, lev_ss, lev_rs, mig_ss, mig_rs, own_ss,
 ):
     me = lax.axis_index("dom")
     up = lax.rem(me + 1, n)
@@ -158,15 +158,31 @@
             device_id_type=MESH,
         )
 
-    def state_copy(target, source):
+    def state_copy(kind, target, source):
+        src, dst = ((packed_level, landed_level), (packed_flow, landed_flow))[kind]
         return pltpu.make_async_remote_copy(
-            src_ref=packed.at[target],
-            dst_ref=landed.at[source],
-            send_sem=mig_ss.at[target],
-            recv_sem=mig_rs.at[source],
+            src_ref=src.at[target],
+            dst_ref=dst.at[source],
+            send_sem=mig_ss.at[kind, target],
+            recv_sem=mig_rs.at[kind, source],
             device_id=(target,),
             device_id_type=MESH,
         )
+
+    def own_copy(kind):
+        src, dst = ((packed_level, landed_level), (packed_flow, landed_flow))[kind]
+        return pltpu.make_async_copy(src.at[me], dst.at[me], own_ss.at[kind])
+
+    def migrate(kind, hi, lo):
+        src = (packed_level, packed_flow)[kind]
+        src[...] = (mm(pack[...], hi) + mm(pack[...], lo)).reshape(src.shape)
+
+        def send(i, _):
+            state_copy(kind, partner(i), me).start()
+            return 0
+
+        lax.fori_loop(1, n, send, 0)
+        own_copy(kind).start()
 
     moved = moved_ref[...].astype(f32)
 
@@ -248,7 +264,7 @@
             hot(lanes == chosen).astype(bf16), hot(lane == pos_col).astype(bf16)
         ).astype(bf16)
 
-    def one_step(step, elevation, opening):
+    def one_step(step, elevation, opening, closing):
         x = x_ref[...]
         hi, lo = halves(x)
         for way, rows_out, slot in ((0, slice(half, blocks), 3), (1, slice(0, half), 4)):
@@ -311,6 +327,8 @@
         )
         if opening:
             choose()
+        if closing:
+            migrate(0, hi, lo)
         lev_copy(step, 0).wait_recv()
         lev_copy(step, 1).wait_recv()
         away = [
@@ -324,56 +342,57 @@
         x_ref[:, cells:] = damp * (x[:, cells:] - depth * grad[:, cells:])
         return level
 
-    level = one_step(0, elevation0, True)
-    level = lax.fori_loop(1, steps, lambda s, e: one_step(s, e, False), level)
-
-    state = jnp.concatenate([level, x_ref[...]], axis=1)
-    hi, lo = halves(state)
-    moving = mm(pack[...], hi) + mm(pack[...], lo)
-    packed[...] = moving.reshape(packed.shape)
-    landed[pl.ds(me, 1)] = packed[pl.ds(me, 1)]
-
-    def send_state(i, _):
-        state_copy(partner(i), me).start()
+    level = one_step(0, elevation0, True, False)
+    level = lax.fori_loop(1, steps - 1, lambda s, e: one_step(s, e, False, False), level)
+    one_step(steps - 1, level, False, True)
+    migrate(1, *halves(x_ref[...]))
+
+    def arrived(i, _):
+        source = lax.rem(me + i, n)
+        for kind in (0, 1):
+            state_copy(kind, source, source).wait_recv()
         return 0
 
-    lax.fori_loop(1, n, send_state, 0)
-
-    owner_row = jnp.floor((moved + 0.5) * (1.0 / blocks))
+    lax.fori_loop(1, n, arrived, 0)
+
+    def sent(i, _):
+        target = lax.rem(me + i, n)
+        tile_copy(target, me).wait_send()
+        for kind in (0, 1):
+            state_copy(kind, target, me).wait_send()
+        return 0
+
+    lax.fori_loop(1, n, sent, 0)
+    for kind in (0, 1):
+        own_copy(kind).wait()
+
+    def halo_sent(step, _):
+        for way in (0, 1):
+            div_copy(step, way).wait_send()
+            lev_copy(step, way).wait_send()
+        return 0
+
+    lax.fori_loop(0, steps, halo_sent, 0)
+
+
+def settle(slots, moved_ref, landed_level, landed_flow, level_out, flow_out):
+    blocks, cells = level_out.shape
+    places = landed_level.shape[0]
+    square = (blocks, blocks)
+    sub, lane = iota(square, 0), iota(square, 1)
+    owner_row = jnp.floor((moved_ref[...].astype(f32) + 0.5) * (1.0 / blocks))
     owner_col = jnp.sum(jnp.where(sub == lane, owner_row, 0.0), axis=1, keepdims=True)
     ahead = jnp.sum(
         jnp.where(lane < sub, hot(owner_row == owner_col), 0.0), axis=1, keepdims=True
     )
     where_from = owner_col * float(slots) + ahead
-    unpack = hot(iota((blocks, n * slots), 1) == where_from).astype(bf16)
-
-    def state_done(i, _):
-        source = lax.rem(me + i, n)
-        state_copy(source, source).wait_recv()
-        return 0
-
-    lax.fori_loop(1, n, state_done, 0)
-    hi, lo = halves(landed[...].reshape(n * slots, 3 * cells))
-    result = mm(unpack, hi) + mm(unpack, lo)
-    level_out[...] = result[:, :cells]
-    flow_out[pl.ds(0, blocks, 2), :] = result[:, cells : 2 * cells]
-    flow_out[pl.ds(1, blocks, 2), :] = result[:, 2 * cells :]
-
-    def sent(i, _):
-        target = lax.rem(me + i, n)
-        tile_copy(target, me).wait_send()
-        state_copy(target, me).wait_send()
-        return 0
-
-    lax.fori_loop(1, n, sent, 0)
-
-    def halo_sent(step, _):
-        for way in (0, 1):
-            div_copy(step, way).wait_send()
-            lev_copy(step, way).wait_send()
-        return 0
-
-    lax.fori_loop(0, steps, halo_sent, 0)
+    unpack = hot(iota((blocks, places), 1) == where_from).astype(bf16)
+    hi, lo = halves(landed_level[...])
+    level_out[...] = mm(unpack, hi) + mm(unpack, lo)
+    hi, lo = halves(landed_flow[...])
+    flow = mm(unpack, hi) + mm(unpack, lo)
+    flow_out[pl.ds(0, blocks, 2), :] = flow[:, :cells]
+    flow_out[pl.ds(1, blocks, 2), :] = flow[:, cells:]
 
 
 def local(
@@ -399,14 +418,14 @@
     slots = -(-portion // 8) * 8
     tall = -(-(steps + blocks // width) // 8) * 8
     vmem, dma = pltpu.VMEM, pltpu.SemaphoreType.DMA
-    level, flow = pl.pallas_call(
+    landed_level, landed_flow = pl.pallas_call(
         functools.partial(kernel, n, slots),
         out_shape=(
-            jax.ShapeDtypeStruct((blocks, cells), f32),
-            jax.ShapeDtypeStruct((2 * blocks, cells), f32),
+            jax.ShapeDtypeStruct((n, slots, cells), f32),
+            jax.ShapeDtypeStruct((n, slots, wide), f32),
         ),
         in_specs=[pl.BlockSpec(memory_space=pl.ANY)] * 12,
-        out_specs=(pl.BlockSpec(memory_space=vmem),) * 2,
+        out_specs=(pl.BlockSpec(memory_space=pl.ANY),) * 2,
         scratch_shapes=[
             vmem((blocks, cells), f32),
             vmem((2 * blocks, cells), f32),
@@ -437,8 +456,8 @@
             vmem((steps, blocks, cells), f32),
             vmem((steps, 2, half, cells), f32),
             vmem((n * slots, blocks), bf16),
-            vmem((n, slots, 3 * cells), f32),
-            vmem((n, slots, 3 * cells), f32),
+            vmem((n, slots, cells), f32),
+            vmem((n, slots, wide), f32),
             dma((12,)),
             dma((n,)),
             dma((n,)),
@@ -446,8 +465,9 @@
             dma((steps, 2)),
             dma((steps, 2)),
             dma((steps, 2)),
-            dma((n,)),
-            dma((n,)),
+            dma((2, n)),
+            dma((2, n)),
+            dma((2,)),
         ],
         compiler_params=pltpu.CompilerParams(
             collective_id=0, has_side_effects=True, vmem_limit_bytes=60 * 1024 * 1024
@@ -466,6 +486,21 @@
         boundary_source.reshape(1, -1),
         series,
         moved_from.reshape(1, -1),
+    )
+    level, flow = pl.pallas_call(
+        functools.partial(settle, slots),
+        out_shape=(
+            jax.ShapeDtypeStruct((blocks, cells), f32),
+            jax.ShapeDtypeStruct((2 * blocks, cells), f32),
+        ),
+        in_specs=[pl.BlockSpec(memory_space=vmem)] * 3,
+        out_specs=(pl.BlockSpec(memory_space=vmem),) * 2,
+        compiler_params=pltpu.CompilerParams(vmem_limit_bytes=60 * 1024 * 1024),
+        name="settle",
+    )(
+        moved_from.reshape(1, -1),
+        landed_level.reshape(n * slots, cells),
+        landed_flow.reshape(n * slots, wide),
     )
     return level, flow.reshape(blocks, 2, cells)
 

time: 66 us -> 62.9 us (0.953)
  the two profiles are of different devices: /device:TPU:0 before, /device:TPU:9 now
where the time goes in v2:
time: 62.9 us; the launch traced here: 62.7 us
  Pallas kernels  62.1 us (99%)
  between operations  0.64 us (1%)
    pallas_call x1, Pallas kernels, local(): pl.pallas_call(functools.partial(kernel, n, slots), out_shape=(jax.ShapeD...  59.6 us
    pallas_call x1, Pallas kernels, local(): pl.pallas_call(functools.partial(settle, slots), out_shape=(jax.ShapeDtyp...  2.46 us

profile of v2, /device:TPU:9, one launch (start us, length us, event | category | flops | bytes accessed | tf_op | source)
XLA Modules:
  0.0 62.7 jit_solution(333463136864915444)
XLA Ops:
  0.6 59.6 %surge.1 = (f32[32,16,128]{2,1,0:T(8,128)}, f32[32,16,256]{2,1,0:T(8,128)}) custom-call(f32[256,128]{1,0:T(8,128)} %elev_hbm.1, f32[512,128]{1,0:T(8,128)} %bitcast.13, f32[256,128]{1,0:T(8,128)} %depth_hbm.1, f32[256,128]{1,0:T(8,128)} %drag_hbm.1, f32[1280,128]{1,0:T(8,128)} %bitcast.10, f32[640,256]{1,0:T(8,128)} %bitcast.11, s32[4,256]{1,0:T(4,128)} %bitcast.17, ...), custom_call_target="tpu_custom_call" | custom-call | tf_op jit(solution)/shard_map/surge/pallas_call | solution.py:421
  60.3 2.5 %settle.1 = (f32[256,128]{1,0:T(8,128)}, f32[512,128]{1,0:T(8,128)}) custom-call(s32[1,256]{1,0:T(1,128)} %bitcast.16, f32[512,128]{1,0:T(8,128)} %bitcast.14, f32[512,256]{1,0:T(8,128)} %bitcast.12), custom_call_target="tpu_custom_call" | custom-call | tf_op jit(solution)/shard_map/settle/pallas_call | solution.py:490

commit v3 on v2

--- a/solution.py
+++ b/solution.py
@@ -41,13 +41,12 @@
     landed_level, landed_flow,
     elev_ref, mom_ref, depth_ref, drag_ref, divw_ref, gradw_ref, nb_ref, wet_ref,
     cells_ref, source_ref, series_ref, moved_ref,
-    meta, gathered, x_ref, dw_hi, dw_lo, gw_hi, gw_lo, damp_ref, depth_p, near_ref,
+    meta, gathered, x_ref, dl_hi, dl_lo, ds_hi, ds_lo, gl_hi, gl_lo, gs_hi, gs_lo,
+    damp_ref, depth_p, near_rows, near_cols, div_ref, grad_ref,
     force_ref, relax_ref, div_send, div_recv, lev_send, lev_recv, pack, packed_level, packed_flow,
     in_ss, meta_ss, meta_rs, div_ss, div_rs, lev_ss, lev_rs, mig_ss, mig_rs, own_ss,
 ):
     me = lax.axis_index("dom")
-    up = lax.rem(me + 1, n)
-    down = lax.rem(me + n - 1, n)
     steps, width = series_ref.shape
     blocks, cells = elev_ref.shape
     half = blocks // 2
@@ -92,6 +91,11 @@
 
     def sl(k, size):
         return slice(k * size, (k + 1) * size)
+
+    near_half, far_half = 1 - lax.rem(me, 2), lax.rem(me, 2)
+
+    def rows_of(h):
+        return pl.ds(pl.multiple_of(h * half, half), half)
 
     for copy in inputs[:6]:
         copy.wait()
@@ -127,33 +131,39 @@
     depth_p[...] = field[:, 3 * cells : 4 * cells]
     damping = 1.0 / (1.0 + field[:, 4 * cells :])
     inputs[10].wait()
-    hi, lo = halves(divw_ref[...])
-    dw_hi[...] = hi
-    dw_lo[...] = lo
-
-    def halo(send, recv, ss, rs, step, way):
+    for half_w, local_w, send_w in zip(halves(divw_ref[...]), (dl_hi, dl_lo), (ds_hi, ds_lo)):
+        slot = [half_w[sl(k, wide), :] for k in range(5)]
+        local_w[0] = jnp.concatenate([slot[0], slot[1]], axis=1)
+        for h in (0, 1):
+            local_w[1 + h] = jnp.concatenate([slot[2], slot[3 + h]], axis=1)
+            send_w[h] = slot[4 - h]
+
+    def halo(send, recv, ss, rs, step, h):
         return pltpu.make_async_remote_copy(
             src_ref=send,
-            dst_ref=recv.at[step, way],
-            send_sem=ss.at[step, way],
-            recv_sem=rs.at[step, way],
-            device_id=((up, down)[way],),
+            dst_ref=recv.at[step, 1 - h],
+            send_sem=ss.at[step, h],
+            recv_sem=rs.at[step, 1 - h],
+            device_id=(lax.rem(me + 2 * h - 1 + n, n),),
             device_id_type=MESH,
         )
 
-    def div_copy(step, way):
-        return halo(div_send.at[step, way], div_recv, div_ss, div_rs, step, way)
-
-    def lev_copy(step, way):
-        rows_out = (pl.ds(half, half), pl.ds(0, half))[way]
-        return halo(lev_send.at[step, rows_out], lev_recv, lev_ss, lev_rs, step, way)
+    def div_copy(step, h):
+        return halo(div_send.at[step, h], div_recv, div_ss, div_rs, step, h)
+
+    def lev_copy(step, h):
+        return halo(lev_send.at[step + 1, rows_of(h)], lev_recv, lev_ss, lev_rs, step, h)
+
+    def shed(step, h):
+        hi, lo = halves(x_ref[rows_of(h), :])
+        div_send[step, h] = mm3(hi, lo, ds_hi[h], ds_lo[h])
 
     def tile_copy(target, source):
         return pltpu.make_async_remote_copy(
             src_ref=meta,
             dst_ref=gathered.at[source],
-            send_sem=meta_ss.at[target],
-            recv_sem=meta_rs.at[source],
+            send_sem=meta_ss,
+            recv_sem=meta_rs,
             device_id=(target,),
             device_id_type=MESH,
         )
@@ -163,11 +173,15 @@
         return pltpu.make_async_remote_copy(
             src_ref=src.at[target],
             dst_ref=dst.at[source],
-            send_sem=mig_ss.at[kind, target],
-            recv_sem=mig_rs.at[kind, source],
+            send_sem=mig_ss.at[kind],
+            recv_sem=mig_rs.at[kind],
             device_id=(target,),
             device_id_type=MESH,
         )
+
+    def all_done(ref, sem):
+        others = ref.at[pl.ds(0, n - 1)]
+        pltpu.make_async_copy(others, others, sem).wait()
 
     def own_copy(kind):
         src, dst = ((packed_level, landed_level), (packed_flow, landed_flow))[kind]
@@ -207,7 +221,9 @@
         vertical = jnp.where(lower_own, nbl[2:3], nbl[3:4])
         for k, ids in enumerate((nbl[0:1], nbl[1:2], vertical)):
             col = jnp.sum(order * place(ids), axis=1, keepdims=True)
-            near_ref[sl(k, blocks), :] = hot(lane == col).astype(bf16)
+            near = hot(lane == col).astype(bf16)
+            near_rows[sl(k, blocks), :] = near
+            near_cols[:, sl(k, blocks)] = near
         wet = wet_ref[...].astype(f32)
         for s in range(steps):
             mask = jnp.sum(order * wet[s : s + 1], axis=1, keepdims=True)
@@ -236,12 +252,7 @@
 
         relax_ref[...] = relax_rate * spread(columns.astype(bf16))
 
-        def tile_done(i, _):
-            source = lax.rem(me + i, n)
-            tile_copy(source, source).wait_recv()
-            return 0
-
-        lax.fori_loop(1, n, tile_done, 0)
+        all_done(gathered, meta_rs)
         tall = meta.shape[0]
         hi, lo = halves(gathered[...].reshape(n * tall, width))
         found = (mm(hi, pick) + mm(lo, pick)).reshape(n, tall, entries)
@@ -264,115 +275,91 @@
             hot(lanes == chosen).astype(bf16), hot(lane == pos_col).astype(bf16)
         ).astype(bf16)
 
-    def one_step(step, elevation, opening, closing):
-        x = x_ref[...]
-        hi, lo = halves(x)
-        for way, rows_out, slot in ((0, slice(half, blocks), 3), (1, slice(0, half), 4)):
-            div_send[step, way] = mm3(
-                hi[rows_out], lo[rows_out], dw_hi[sl(slot, wide), :], dw_lo[sl(slot, wide), :]
-            )
-            if not opening:
-                div_copy(step, way).start()
+    def one_step(step, opening, closing):
         if opening:
             open_up()
-            for way in (0, 1):
-                div_copy(step, way).start()
+            for h in (far_half, near_half):
+                div_copy(step, h).start()
             send_tiles()
-        near = mm(near_ref[...], jnp.concatenate([hi, lo], axis=1)).astype(bf16)
-        three = slice(0, 3 * wide)
-        hi3 = jnp.concatenate([hi, near[:blocks, :wide], near[blocks : 2 * blocks, :wide]], axis=1)
-        lo3 = jnp.concatenate([lo, near[:blocks, wide:], near[blocks : 2 * blocks, wide:]], axis=1)
-        div = mm3(hi3, lo3, dw_hi[three, :], dw_lo[three, :])
-        upper = near[2 * blocks :]
-        div = div + jnp.concatenate(
+        hi, lo = halves(x_ref[...])
+        first = mm3(hi, lo, dl_hi[0], dl_lo[0])
+        second = jnp.concatenate(
             [
-                mm3(
-                    upper[r, :wide], upper[r, wide:], dw_hi[sl(k, wide), :], dw_lo[sl(k, wide), :]
-                )
-                for r, k in ((slice(0, half), 4), (slice(half, blocks), 3))
+                mm3(hi[sl(h, half)], lo[sl(h, half)], dl_hi[1 + h], dl_lo[1 + h])
+                for h in (0, 1)
             ],
             axis=0,
         )
+        parts = jnp.concatenate([first[:, cells:], second[:, :cells], second[:, cells:]], axis=0)
+        parts = mm(near_cols[...], jnp.concatenate(halves(parts), axis=1))
+        div_ref[...] = first[:, :cells] + (parts[:, :cells] + parts[:, cells:])
         if opening:
             boundary()
-        div_copy(step, 0).wait_recv()
-        div_copy(step, 1).wait_recv()
-        div = div + jnp.concatenate([div_recv[step, 0], div_recv[step, 1]], axis=0)
-        level = elevation - damp_ref[step, :, :cells] * div
-        level = level + relax_ref[...] * (force_ref[step] - level)
-        lev_send[step] = level
-        lev_copy(step, 0).start()
-        lev_copy(step, 1).start()
+        for h in (near_half, far_half):
+            r = rows_of(h)
+            div_copy(step, 1 - h).wait_recv()
+            div = div_ref[r, :] + div_recv[step, h]
+            level = lev_send[step, r, :] - damp_ref[step, r, :cells] * div
+            lev_send[step + 1, r, :] = level + relax_ref[r, :] * (force_ref[step, r, :] - level)
+            lev_copy(step, h).start()
         if opening:
             inputs[11].wait()
-            hi, lo = halves(gradw_ref[...])
-            gw_hi[...] = hi
-            gw_lo[...] = lo
-        hi, lo = halves(level)
-        near = mm(near_ref[...], jnp.concatenate([hi, lo], axis=1)).astype(bf16)
-        three = slice(0, 3 * cells)
-        hi3 = jnp.concatenate([hi, near[:blocks, :cells], near[blocks : 2 * blocks, :cells]], axis=1)
-        lo3 = jnp.concatenate([lo, near[:blocks, cells:], near[blocks : 2 * blocks, cells:]], axis=1)
-        grad = mm3(hi3, lo3, gw_hi[three, :], gw_lo[three, :])
-        upper = near[2 * blocks :]
-        grad = grad + jnp.concatenate(
-            [
-                mm3(
-                    upper[r, :cells], upper[r, cells:],
-                    gw_hi[sl(k, cells), :], gw_lo[sl(k, cells), :],
-                )
-                for r, k in ((slice(0, half), 4), (slice(half, blocks), 3))
-            ],
-            axis=0,
-        )
+            for half_w, local_w, away_w in zip(
+                halves(gradw_ref[...]), (gl_hi, gl_lo), (gs_hi, gs_lo)
+            ):
+                slot = [half_w[sl(k, cells), :] for k in range(5)]
+                for h in (0, 1):
+                    local_w[h] = jnp.concatenate(slot[:3] + [slot[4 - h]], axis=0)
+                    away_w[h] = slot[3 + h]
+        hi, lo = halves(lev_send[step + 1])
+        near = mm(near_rows[...], jnp.concatenate([hi, lo], axis=1)).astype(bf16)
+        near = [near[sl(k, blocks)] for k in range(3)]
+        hi4 = jnp.concatenate([hi] + [p[:, :cells] for p in near], axis=1)
+        lo4 = jnp.concatenate([lo] + [p[:, cells:] for p in near], axis=1)
+        for h in (0, 1):
+            r = sl(h, half)
+            grad_ref[r, :] = mm3(hi4[r], lo4[r], gl_hi[h], gl_lo[h])
         if opening:
             choose()
         if closing:
             migrate(0, hi, lo)
-        lev_copy(step, 0).wait_recv()
-        lev_copy(step, 1).wait_recv()
-        away = [
-            mm3(*halves(lev_recv[step, way]), gw_hi[sl(k, cells), :], gw_lo[sl(k, cells), :])
-            for way, k in ((0, 3), (1, 4))
-        ]
-        grad = grad + jnp.concatenate(away, axis=0)
-        depth = depth_p[...]
-        damp = damp_ref[step, :, cells:]
-        x_ref[:, :cells] = damp * (x[:, :cells] - depth * grad[:, :cells])
-        x_ref[:, cells:] = damp * (x[:, cells:] - depth * grad[:, cells:])
-        return level
-
-    level = one_step(0, elevation0, True, False)
-    level = lax.fori_loop(1, steps - 1, lambda s, e: one_step(s, e, False, False), level)
-    one_step(steps - 1, level, False, True)
+        for h in (near_half, far_half):
+            r = rows_of(h)
+            lev_copy(step, 1 - h).wait_recv()
+            grad = grad_ref[r, :] + mm3(*halves(lev_recv[step, h]), gs_hi[h], gs_lo[h])
+            depth = depth_p[r, :]
+            damp = damp_ref[step, r, cells:]
+            x_ref[r, :cells] = damp * (x_ref[r, :cells] - depth * grad[:, :cells])
+            x_ref[r, cells:] = damp * (x_ref[r, cells:] - depth * grad[:, cells:])
+            if not closing:
+                shed(step + 1, h)
+                div_copy(step + 1, h).start()
+
+    lev_send[0] = elevation0
+    for h in (0, 1):
+        shed(0, h)
+    one_step(0, True, False)
+
+    def middle(step, _):
+        one_step(step, False, False)
+        return 0
+
+    lax.fori_loop(1, steps - 1, middle, 0)
+    one_step(steps - 1, False, True)
     migrate(1, *halves(x_ref[...]))
 
-    def arrived(i, _):
-        source = lax.rem(me + i, n)
-        for kind in (0, 1):
-            state_copy(kind, source, source).wait_recv()
+    def halo_sent(step, _):
+        for h in (0, 1):
+            div_copy(step, h).wait_send()
+            lev_copy(step, h).wait_send()
         return 0
 
-    lax.fori_loop(1, n, arrived, 0)
-
-    def sent(i, _):
-        target = lax.rem(me + i, n)
-        tile_copy(target, me).wait_send()
-        for kind in (0, 1):
-            state_copy(kind, target, me).wait_send()
-        return 0
-
-    lax.fori_loop(1, n, sent, 0)
-    for kind in (0, 1):
+    lax.fori_loop(0, steps, halo_sent, 0)
+    all_done(gathered, meta_ss)
+    for kind, src, dst in ((0, packed_level, landed_level), (1, packed_flow, landed_flow)):
         own_copy(kind).wait()
-
-    def halo_sent(step, _):
-        for way in (0, 1):
-            div_copy(step, way).wait_send()
-            lev_copy(step, way).wait_send()
-        return 0
-
-    lax.fori_loop(0, steps, halo_sent, 0)
+        all_done(src, mig_ss.at[kind])
+        all_done(dst, mig_rs.at[kind])
 
 
 def settle(slots, moved_ref, landed_level, landed_flow, level_out, flow_out):
@@ -442,31 +429,38 @@
             vmem((tall, width), f32),
             vmem((n, tall, width), f32),
             vmem((blocks, wide), f32),
-            vmem((5 * wide, cells), bf16),
-            vmem((5 * wide, cells), bf16),
-            vmem((5 * cells, wide), bf16),
-            vmem((5 * cells, wide), bf16),
+            vmem((3, wide, wide), bf16),
+            vmem((3, wide, wide), bf16),
+            vmem((2, wide, cells), bf16),
+            vmem((2, wide, cells), bf16),
+            vmem((2, 4 * cells, wide), bf16),
+            vmem((2, 4 * cells, wide), bf16),
+            vmem((2, cells, wide), bf16),
+            vmem((2, cells, wide), bf16),
             vmem((steps, blocks, wide), f32),
             vmem((blocks, cells), f32),
             vmem((3 * blocks, blocks), bf16),
+            vmem((blocks, 3 * blocks), bf16),
+            vmem((blocks, cells), f32),
+            vmem((blocks, wide), f32),
             vmem((steps, blocks, cells), f32),
             vmem((blocks, cells), f32),
             vmem((steps, 2, half, cells), f32),
             vmem((steps, 2, half, cells), f32),
-            vmem((steps, blocks, cells), f32),
+            vmem((steps + 1, blocks, cells), f32),
             vmem((steps, 2, half, cells), f32),
             vmem((n * slots, blocks), bf16),
             vmem((n, slots, cells), f32),
             vmem((n, slots, wide), f32),
             dma((12,)),
-            dma((n,)),
-            dma((n,)),
+            dma,
+            dma,
             dma((steps, 2)),
             dma((steps, 2)),
             dma((steps, 2)),
             dma((steps, 2)),
-            dma((2, n)),
-            dma((2, n)),
+            dma((2,)),
+            dma((2,)),
             dma((2,)),
         ],
         compiler_params=pltpu.CompilerParams(

time: 62.9 us -> 59 us (0.938)
  the two profiles are of different devices: /device:TPU:9 before, /device:TPU:0 now
where the time goes in v3:
time: 59 us; the launch traced here: 58.8 us
  Pallas kernels  58.2 us (99%)
  between operations  0.64 us (1%)
    pallas_call x1, Pallas kernels, local(): pl.pallas_call(functools.partial(kernel, n, slots), out_shape=(jax.ShapeD...  55.7 us
    pallas_call x1, Pallas kernels, local(): pl.pallas_call(functools.partial(settle, slots), out_shape=(jax.ShapeDtyp...  2.46 us

profile of v3, /device:TPU:0, one launch (start us, length us, event | category | flops | bytes accessed | tf_op | source)
XLA Modules:
  0.0 58.8 jit_solution(14651526857669517820)
XLA Ops:
  0.6 55.7 %surge.1 = (f32[32,16,128]{2,1,0:T(8,128)}, f32[32,16,256]{2,1,0:T(8,128)}) custom-call(f32[256,128]{1,0:T(8,128)} %elev_hbm.1, f32[512,128]{1,0:T(8,128)} %bitcast.13, f32[256,128]{1,0:T(8,128)} %depth_hbm.1, f32[256,128]{1,0:T(8,128)} %drag_hbm.1, f32[1280,128]{1,0:T(8,128)} %bitcast.10, f32[640,256]{1,0:T(8,128)} %bitcast.11, s32[4,256]{1,0:T(4,128)} %bitcast.17, ...), custom_call_target="tpu_custom_call" | custom-call | tf_op jit(solution)/shard_map/surge/pallas_call | solution.py:408
  56.4 2.5 %settle.1 = (f32[256,128]{1,0:T(8,128)}, f32[512,128]{1,0:T(8,128)}) custom-call(s32[1,256]{1,0:T(1,128)} %bitcast.16, f32[512,128]{1,0:T(8,128)} %bitcast.14, f32[512,256]{1,0:T(8,128)} %bitcast.12), custom_call_target="tpu_custom_call" | custom-call | tf_op jit(solution)/shard_map/settle/pallas_call | solution.py:484

commit v4 on v3

--- a/solution.py
+++ b/solution.py
@@ -41,7 +41,7 @@
     landed_level, landed_flow,
     elev_ref, mom_ref, depth_ref, drag_ref, divw_ref, gradw_ref, nb_ref, wet_ref,
     cells_ref, source_ref, series_ref, moved_ref,
-    meta, gathered, x_ref, dl_hi, dl_lo, ds_hi, ds_lo, gl_hi, gl_lo, gs_hi, gs_lo,
+    meta, gathered, x_ref, dl_hi, dl_lo, ds_both, gl_hi, gl_lo, gs_twice, gs_lo,
     damp_ref, depth_p, near_rows, near_cols, div_ref, grad_ref,
     force_ref, relax_ref, div_send, div_recv, lev_send, lev_recv, pack, packed_level, packed_flow,
     in_ss, meta_ss, meta_rs, div_ss, div_rs, lev_ss, lev_rs, mig_ss, mig_rs, own_ss,
@@ -94,8 +94,12 @@
 
     near_half, far_half = 1 - lax.rem(me, 2), lax.rem(me, 2)
 
-    def rows_of(h):
-        return pl.ds(pl.multiple_of(h * half, half), half)
+    near_pieces = [(near_half, 0, 0, half)]
+    far_pieces = [(far_half, i, i * (half // 2), half // 2) for i in (0, 1)]
+
+    def rows_of(piece):
+        h, _, first, size = piece
+        return pl.ds(pl.multiple_of(h * half + first, half // 2), size)
 
     for copy in inputs[:6]:
         copy.wait()
@@ -131,32 +135,44 @@
     depth_p[...] = field[:, 3 * cells : 4 * cells]
     damping = 1.0 / (1.0 + field[:, 4 * cells :])
     inputs[10].wait()
-    for half_w, local_w, send_w in zip(halves(divw_ref[...]), (dl_hi, dl_lo), (ds_hi, ds_lo)):
+    hi, lo = halves(divw_ref[...])
+    for half_w, local_w in ((hi, dl_hi), (lo, dl_lo)):
         slot = [half_w[sl(k, wide), :] for k in range(5)]
         local_w[0] = jnp.concatenate([slot[0], slot[1]], axis=1)
         for h in (0, 1):
             local_w[1 + h] = jnp.concatenate([slot[2], slot[3 + h]], axis=1)
-            send_w[h] = slot[4 - h]
-
-    def halo(send, recv, ss, rs, step, h):
+    for h in (0, 1):
+        ds_both[h] = jnp.concatenate([hi[sl(4 - h, wide), :], lo[sl(4 - h, wide), :]], axis=1)
+
+    def halo(src, recv, ss, rs, step, piece):
+        h, i, first, size = piece
         return pltpu.make_async_remote_copy(
-            src_ref=send,
-            dst_ref=recv.at[step, 1 - h],
-            send_sem=ss.at[step, h],
-            recv_sem=rs.at[step, 1 - h],
+            src_ref=src,
+            dst_ref=recv.at[step, 1 - h, pl.ds(first, size)],
+            send_sem=ss.at[step, h, i],
+            recv_sem=rs.at[step, 1 - h, i],
             device_id=(lax.rem(me + 2 * h - 1 + n, n),),
             device_id_type=MESH,
         )
 
-    def div_copy(step, h):
-        return halo(div_send.at[step, h], div_recv, div_ss, div_rs, step, h)
-
-    def lev_copy(step, h):
-        return halo(lev_send.at[step + 1, rows_of(h)], lev_recv, lev_ss, lev_rs, step, h)
-
-    def shed(step, h):
-        hi, lo = halves(x_ref[rows_of(h), :])
-        div_send[step, h] = mm3(hi, lo, ds_hi[h], ds_lo[h])
+    def div_copy(step, piece):
+        h, _, first, size = piece
+        src = div_send.at[step, h, pl.ds(first, size)]
+        return halo(src, div_recv, div_ss, div_rs, step, piece)
+
+    def lev_copy(step, piece):
+        src = lev_send.at[step + 1, rows_of(piece)]
+        return halo(src, lev_recv, lev_ss, lev_rs, step, piece)
+
+    def facing(piece):
+        return (1 - piece[0],) + piece[1:]
+
+    def shed(step, piece):
+        h, _, first, size = piece
+        hi, lo = halves(x_ref[rows_of(piece), :])
+        both = mm(hi, ds_both[h])
+        rest = mm(lo, ds_both[h, :, :cells])
+        div_send[step, h, first : first + size] = both[:, :cells] + (both[:, cells:] + rest)
 
     def tile_copy(target, source):
         return pltpu.make_async_remote_copy(
@@ -278,8 +294,8 @@
     def one_step(step, opening, closing):
         if opening:
             open_up()
-            for h in (far_half, near_half):
-                div_copy(step, h).start()
+            for piece in far_pieces + near_pieces:
+                div_copy(step, piece).start()
             send_tiles()
         hi, lo = halves(x_ref[...])
         first = mm3(hi, lo, dl_hi[0], dl_lo[0])
@@ -295,23 +311,27 @@
         div_ref[...] = first[:, :cells] + (parts[:, :cells] + parts[:, cells:])
         if opening:
             boundary()
-        for h in (near_half, far_half):
-            r = rows_of(h)
-            div_copy(step, 1 - h).wait_recv()
-            div = div_ref[r, :] + div_recv[step, h]
+        for piece in near_pieces + far_pieces:
+            h, _, first, size = piece
+            r = rows_of(piece)
+            div_copy(step, facing(piece)).wait_recv()
+            div = div_ref[r, :] + div_recv[step, h, first : first + size]
             level = lev_send[step, r, :] - damp_ref[step, r, :cells] * div
             lev_send[step + 1, r, :] = level + relax_ref[r, :] * (force_ref[step, r, :] - level)
-            lev_copy(step, h).start()
+            lev_copy(step, piece).start()
         if opening:
             inputs[11].wait()
-            for half_w, local_w, away_w in zip(
-                halves(gradw_ref[...]), (gl_hi, gl_lo), (gs_hi, gs_lo)
-            ):
+            hi, lo = halves(gradw_ref[...])
+            for half_w, local_w in ((hi, gl_hi), (lo, gl_lo)):
                 slot = [half_w[sl(k, cells), :] for k in range(5)]
                 for h in (0, 1):
                     local_w[h] = jnp.concatenate(slot[:3] + [slot[4 - h]], axis=0)
-                    away_w[h] = slot[3 + h]
+            for h in (0, 1):
+                gs_twice[h] = jnp.concatenate([hi[sl(3 + h, cells), :]] * 2, axis=0)
+                gs_lo[h] = lo[sl(3 + h, cells), :]
         hi, lo = halves(lev_send[step + 1])
+        if closing:
+            migrate(0, hi, lo)
         near = mm(near_rows[...], jnp.concatenate([hi, lo], axis=1)).astype(bf16)
         near = [near[sl(k, blocks)] for k in range(3)]
         hi4 = jnp.concatenate([hi] + [p[:, :cells] for p in near], axis=1)
@@ -321,23 +341,24 @@
             grad_ref[r, :] = mm3(hi4[r], lo4[r], gl_hi[h], gl_lo[h])
         if opening:
             choose()
-        if closing:
-            migrate(0, hi, lo)
-        for h in (near_half, far_half):
-            r = rows_of(h)
-            lev_copy(step, 1 - h).wait_recv()
-            grad = grad_ref[r, :] + mm3(*halves(lev_recv[step, h]), gs_hi[h], gs_lo[h])
+        for piece in near_pieces + far_pieces:
+            h, _, first, size = piece
+            r = rows_of(piece)
+            lev_copy(step, facing(piece)).wait_recv()
+            hi, lo = halves(lev_recv[step, h, first : first + size])
+            grad = mm(jnp.concatenate([hi, lo], axis=1), gs_twice[h]) + mm(hi, gs_lo[h])
+            grad = grad_ref[r, :] + grad
             depth = depth_p[r, :]
             damp = damp_ref[step, r, cells:]
             x_ref[r, :cells] = damp * (x_ref[r, :cells] - depth * grad[:, :cells])
             x_ref[r, cells:] = damp * (x_ref[r, cells:] - depth * grad[:, cells:])
             if not closing:
-                shed(step + 1, h)
-                div_copy(step + 1, h).start()
+                shed(step + 1, piece)
+                div_copy(step + 1, piece).start()
 
     lev_send[0] = elevation0
-    for h in (0, 1):
-        shed(0, h)
+    for piece in far_pieces + near_pieces:
+        shed(0, piece)
     one_step(0, True, False)
 
     def middle(step, _):
@@ -349,9 +370,9 @@
     migrate(1, *halves(x_ref[...]))
 
     def halo_sent(step, _):
-        for h in (0, 1):
-            div_copy(step, h).wait_send()
-            lev_copy(step, h).wait_send()
+        for piece in near_pieces + far_pieces:
+            div_copy(step, piece).wait_send()
+            lev_copy(step, piece).wait_send()
         return 0
 
     lax.fori_loop(0, steps, halo_sent, 0)
@@ -431,11 +452,10 @@
             vmem((blocks, wide), f32),
             vmem((3, wide, wide), bf16),
             vmem((3, wide, wide), bf16),
-            vmem((2, wide, cells), bf16),
-            vmem((2, wide, cells), bf16),
+            vmem((2, wide, wide), bf16),
             vmem((2, 4 * cells, wide), bf16),
             vmem((2, 4 * cells, wide), bf16),
-            vmem((2, cells, wide), bf16),
+            vmem((2, wide, wide), bf16),
             vmem((2, cells, wide), bf16),
             vmem((steps, blocks, wide), f32),
             vmem((blocks, cells), f32),
@@ -455,10 +475,10 @@
             dma((12,)),
             dma,
             dma,
-            dma((steps, 2)),
-            dma((steps, 2)),
-            dma((steps, 2)),
-            dma((steps, 2)),
+            dma((steps, 2, 2)),
+            dma((steps, 2, 2)),
+            dma((steps, 2, 2)),
+            dma((steps, 2, 2)),
             dma((2,)),
             dma((2,)),
             dma((2,)),

time: 59 us -> 58 us (0.983)
  Pallas kernels: 58.2 us -> 57.2 us
    pallas_call x1, Pallas kernels: 55.7 us -> 54.7 us  [local(): pl.pallas_call(functools.partial(kernel, n, slots), out_shape=(jax.ShapeD...]
where the time goes in v4:
time: 58 us; the launch traced here: 57.8 us
  Pallas kernels  57.2 us (99%)
  between operations  0.64 us (1%)
    pallas_call x1, Pallas kernels, local(): pl.pallas_call(functools.partial(kernel, n, slots), out_shape=(jax.ShapeD...  54.7 us
    pallas_call x1, Pallas kernels, local(): pl.pallas_call(functools.partial(settle, slots), out_shape=(jax.ShapeDtyp...  2.46 us

profile of v4, /device:TPU:0, one launch (start us, length us, event | category | flops | bytes accessed | tf_op | source)
XLA Modules:
  0.0 57.8 jit_solution(2290390074354319866)
XLA Ops:
  0.6 54.7 %surge.1 = (f32[32,16,128]{2,1,0:T(8,128)}, f32[32,16,256]{2,1,0:T(8,128)}) custom-call(f32[256,128]{1,0:T(8,128)} %elev_hbm.1, f32[512,128]{1,0:T(8,128)} %bitcast.13, f32[256,128]{1,0:T(8,128)} %depth_hbm.1, f32[256,128]{1,0:T(8,128)} %drag_hbm.1, f32[1280,128]{1,0:T(8,128)} %bitcast.10, f32[640,256]{1,0:T(8,128)} %bitcast.11, s32[4,256]{1,0:T(4,128)} %bitcast.17, ...), custom_call_target="tpu_custom_call" | custom-call | tf_op jit(solution)/shard_map/surge/pallas_call | solution.py:429
  55.4 2.5 %settle.1 = (f32[256,128]{1,0:T(8,128)}, f32[512,128]{1,0:T(8,128)}) custom-call(s32[1,256]{1,0:T(1,128)} %bitcast.16, f32[512,128]{1,0:T(8,128)} %bitcast.14, f32[512,256]{1,0:T(8,128)} %bitcast.12), custom_call_target="tpu_custom_call" | custom-call | tf_op jit(solution)/shard_map/settle/pallas_call | solution.py:504

commit v5 on v4

--- a/solution.py
+++ b/solution.py
@@ -85,9 +85,15 @@
 
     lax.fori_loop(1, n, greet, 0)
 
+    bits = n.bit_length() - 1
+    flips = [(1 - 2 * lax.rem(lax.div(me, 1 << k), 2)) * (1 << k) for k in range(bits)]
+
     def partner(i):
         j = i - 1
-        return lax.rem(me + (j + 1) // 2 + (1 - j % 2) * (n // 2), n)
+        m = lax.div(j + 1, 2) + (1 - lax.rem(j, 2)) * (n // 2)
+        if n != 1 << bits:
+            return lax.rem(me + m, n)
+        return me + sum(lax.rem(lax.div(m, 1 << k), 2) * flips[k] for k in range(bits))
 
     def sl(k, size):
         return slice(k * size, (k + 1) * size)
@@ -273,9 +279,13 @@
         hi, lo = halves(gathered[...].reshape(n * tall, width))
         found = (mm(hi, pick) + mm(lo, pick)).reshape(n, tall, entries)
         found = jnp.sum(jnp.where(iota(found.shape, 0) == chunk[None], found, 0.0), axis=0)
-        for s in range(steps):
+
+        def force(s):
             hi, lo = halves(columns * found[s : s + 1])
             force_ref[s] = spread(hi) + spread(lo)
+
+        force(0)
+        return force
 
     def choose():
         everyone = gathered[...]
@@ -310,7 +320,7 @@
         parts = mm(near_cols[...], jnp.concatenate(halves(parts), axis=1))
         div_ref[...] = first[:, :cells] + (parts[:, :cells] + parts[:, cells:])
         if opening:
-            boundary()
+            force = boundary()
         for piece in near_pieces + far_pieces:
             h, _, first, size = piece
             r = rows_of(piece)
@@ -340,6 +350,8 @@
             r = sl(h, half)
             grad_ref[r, :] = mm3(hi4[r], lo4[r], gl_hi[h], gl_lo[h])
         if opening:
+            for later in range(1, steps):
+                force(later)
             choose()
         for piece in near_pieces + far_pieces:
             h, _, first, size = piece
@@ -383,11 +395,29 @@
         all_done(dst, mig_rs.at[kind])
 
 
-def settle(slots, moved_ref, landed_level, landed_flow, level_out, flow_out):
-    blocks, cells = level_out.shape
+def settle(
+    slots, moved_hbm, level_hbm, flow_hbm, level_out, flow_out,
+    moved_ref, landed_level, landed_flow, level_ref, flow_ref, sem,
+):
+    copies = [
+        pltpu.make_async_copy(src, dst, sem.at[i])
+        for i, (src, dst) in enumerate(
+            (
+                (moved_hbm, moved_ref),
+                (level_hbm, landed_level),
+                (flow_hbm, landed_flow),
+                (level_ref, level_out),
+                (flow_ref, flow_out),
+            )
+        )
+    ]
+    for copy in copies[:3]:
+        copy.start()
+    blocks, cells = level_ref.shape
     places = landed_level.shape[0]
     square = (blocks, blocks)
     sub, lane = iota(square, 0), iota(square, 1)
+    copies[0].wait()
     owner_row = jnp.floor((moved_ref[...].astype(f32) + 0.5) * (1.0 / blocks))
     owner_col = jnp.sum(jnp.where(sub == lane, owner_row, 0.0), axis=1, keepdims=True)
     ahead = jnp.sum(
@@ -395,12 +425,19 @@
     )
     where_from = owner_col * float(slots) + ahead
     unpack = hot(iota((blocks, places), 1) == where_from).astype(bf16)
+    copies[1].wait()
     hi, lo = halves(landed_level[...])
-    level_out[...] = mm(unpack, hi) + mm(unpack, lo)
+    both = mm(unpack, jnp.concatenate([hi, lo], axis=1))
+    level_ref[...] = both[:, :cells] + both[:, cells:]
+    copies[3].start()
+    copies[2].wait()
     hi, lo = halves(landed_flow[...])
     flow = mm(unpack, hi) + mm(unpack, lo)
-    flow_out[pl.ds(0, blocks, 2), :] = flow[:, :cells]
-    flow_out[pl.ds(1, blocks, 2), :] = flow[:, cells:]
+    flow_ref[pl.ds(0, blocks, 2), :] = flow[:, :cells]
+    flow_ref[pl.ds(1, blocks, 2), :] = flow[:, cells:]
+    copies[4].start()
+    copies[3].wait()
+    copies[4].wait()
 
 
 def local(
@@ -507,8 +544,16 @@
             jax.ShapeDtypeStruct((blocks, cells), f32),
             jax.ShapeDtypeStruct((2 * blocks, cells), f32),
         ),
-        in_specs=[pl.BlockSpec(memory_space=vmem)] * 3,
-        out_specs=(pl.BlockSpec(memory_space=vmem),) * 2,
+        in_specs=[pl.BlockSpec(memory_space=pl.ANY)] * 3,
+        out_specs=(pl.BlockSpec(memory_space=pl.ANY),) * 2,
+        scratch_shapes=[
+            vmem((1, blocks), jnp.int32),
+            vmem((n * slots, cells), f32),
+            vmem((n * slots, wide), f32),
+            vmem((blocks, cells), f32),
+            vmem((2 * blocks, cells), f32),
+            dma((5,)),
+        ],
         compiler_params=pltpu.CompilerParams(vmem_limit_bytes=60 * 1024 * 1024),
         name="settle",
     )(

time: 58 us -> 58.2 us (level)
  no operation moved by 1% of the time
where the time goes in v5:
time: 58.2 us; the launch traced here: 58 us
  Pallas kernels  57.4 us (99%)
  between operations  0.64 us (1%)
    pallas_call x1, Pallas kernels, local(): pl.pallas_call(functools.partial(kernel, n, slots), out_shape=(jax.ShapeD...  55 us
    pallas_call x1, Pallas kernels, local(): pl.pallas_call(functools.partial(settle, slots), out_shape=(jax.ShapeDtyp...  2.37 us

profile of v5, /device:TPU:0, one launch (start us, length us, event | category | flops | bytes accessed | tf_op | source)
XLA Modules:
  0.0 58.0 jit_solution(13103888557895378059)
XLA Ops:
  0.6 55.0 %surge.1 = (f32[32,16,128]{2,1,0:T(8,128)}, f32[32,16,256]{2,1,0:T(8,128)}) custom-call(f32[256,128]{1,0:T(8,128)} %elev_hbm.1, f32[512,128]{1,0:T(8,128)} %bitcast.13, f32[256,128]{1,0:T(8,128)} %depth_hbm.1, f32[256,128]{1,0:T(8,128)} %drag_hbm.1, f32[1280,128]{1,0:T(8,128)} %bitcast.10, f32[640,256]{1,0:T(8,128)} %bitcast.11, s32[4,256]{1,0:T(4,128)} %bitcast.17, ...), custom_call_target="tpu_custom_call" | custom-call | tf_op jit(solution)/shard_map/surge/pallas_call | solution.py:466
  55.7 2.4 %settle.1 = (f32[256,128]{1,0:T(8,128)}, f32[512,128]{1,0:T(8,128)}) custom-call(s32[1,256]{1,0:T(1,128)} %bitcast.16, f32[512,128]{1,0:T(8,128)} %bitcast.14, f32[512,256]{1,0:T(8,128)} %bitcast.12), custom_call_target="tpu_custom_call" | custom-call | tf_op jit(solution)/shard_map/settle/pallas_call | solution.py:541

commit v6 on v5

--- a/solution.py
+++ b/solution.py
@@ -122,33 +122,17 @@
     order = hot(sub == pos_row)
     order16 = order.astype(bf16)
 
-    for copy in inputs[6:10]:
-        copy.wait()
-    field = jnp.concatenate(
-        [
-            mom_ref[pl.ds(0, blocks, 2), :],
-            mom_ref[pl.ds(1, blocks, 2), :],
-            elev_ref[...],
-            depth_ref[...],
-            drag_ref[...],
-        ],
-        axis=1,
+    inputs[6].wait()
+    hi, lo = halves(
+        jnp.concatenate(
+            [mom_ref[pl.ds(0, blocks, 2), :], mom_ref[pl.ds(1, blocks, 2), :]], axis=1
+        )
     )
-    hi, lo = halves(field)
-    field = mm(order16, hi) + mm(order16, lo)
-    x_ref[...] = field[:, :wide]
-    elevation0 = field[:, wide : 3 * cells]
-    depth_p[...] = field[:, 3 * cells : 4 * cells]
-    damping = 1.0 / (1.0 + field[:, 4 * cells :])
+    x_ref[...] = mm(order16, hi) + mm(order16, lo)
     inputs[10].wait()
-    hi, lo = halves(divw_ref[...])
-    for half_w, local_w in ((hi, dl_hi), (lo, dl_lo)):
-        slot = [half_w[sl(k, wide), :] for k in range(5)]
-        local_w[0] = jnp.concatenate([slot[0], slot[1]], axis=1)
-        for h in (0, 1):
-            local_w[1 + h] = jnp.concatenate([slot[2], slot[3 + h]], axis=1)
     for h in (0, 1):
-        ds_both[h] = jnp.concatenate([hi[sl(4 - h, wide), :], lo[sl(4 - h, wide), :]], axis=1)
+        hi, lo = halves(divw_ref[sl(4 - h, wide), :])
+        ds_both[h] = jnp.concatenate([hi, lo], axis=1)
 
     def halo(src, recv, ss, rs, step, piece):
         h, i, first, size = piece
@@ -246,6 +230,19 @@
             near = hot(lane == col).astype(bf16)
             near_rows[sl(k, blocks), :] = near
             near_cols[:, sl(k, blocks)] = near
+        for copy in inputs[7:10]:
+            copy.wait()
+        hi, lo = halves(jnp.concatenate([elev_ref[...], depth_ref[...], drag_ref[...]], axis=1))
+        field = mm(order16, hi) + mm(order16, lo)
+        lev_send[0] = field[:, :cells]
+        depth_p[...] = field[:, cells : 2 * cells]
+        damping = 1.0 / (1.0 + field[:, 2 * cells :])
+        hi, lo = halves(divw_ref[...])
+        for half_w, local_w in ((hi, dl_hi), (lo, dl_lo)):
+            slot = [half_w[sl(k, wide), :] for k in range(5)]
+            local_w[0] = jnp.concatenate([slot[0], slot[1]], axis=1)
+            for h in (0, 1):
+                local_w[1 + h] = jnp.concatenate([slot[2], slot[3 + h]], axis=1)
         wet = wet_ref[...].astype(f32)
         for s in range(steps):
             mask = jnp.sum(order * wet[s : s + 1], axis=1, keepdims=True)
@@ -301,8 +298,11 @@
             hot(lanes == chosen).astype(bf16), hot(lane == pos_col).astype(bf16)
         ).astype(bf16)
 
-    def one_step(step, opening, closing):
-        if opening:
+    def one_step(step):
+        opening, closing = step == 0, step == steps - 1
+
+        @pl.when(opening)
+        def _():
             open_up()
             for piece in far_pieces + near_pieces:
                 div_copy(step, piece).start()
@@ -319,8 +319,12 @@
         parts = jnp.concatenate([first[:, cells:], second[:, :cells], second[:, cells:]], axis=0)
         parts = mm(near_cols[...], jnp.concatenate(halves(parts), axis=1))
         div_ref[...] = first[:, :cells] + (parts[:, :cells] + parts[:, cells:])
-        if opening:
+        @pl.when(opening)
+        def _():
             force = boundary()
+            for later in range(1, steps):
+                force(later)
+
         for piece in near_pieces + far_pieces:
             h, _, first, size = piece
             r = rows_of(piece)
@@ -329,7 +333,8 @@
             level = lev_send[step, r, :] - damp_ref[step, r, :cells] * div
             lev_send[step + 1, r, :] = level + relax_ref[r, :] * (force_ref[step, r, :] - level)
             lev_copy(step, piece).start()
-        if opening:
+        @pl.when(opening)
+        def _():
             inputs[11].wait()
             hi, lo = halves(gradw_ref[...])
             for half_w, local_w in ((hi, gl_hi), (lo, gl_lo)):
@@ -340,8 +345,11 @@
                 gs_twice[h] = jnp.concatenate([hi[sl(3 + h, cells), :]] * 2, axis=0)
                 gs_lo[h] = lo[sl(3 + h, cells), :]
         hi, lo = halves(lev_send[step + 1])
-        if closing:
+
+        @pl.when(closing)
+        def _():
             migrate(0, hi, lo)
+
         near = mm(near_rows[...], jnp.concatenate([hi, lo], axis=1)).astype(bf16)
         near = [near[sl(k, blocks)] for k in range(3)]
         hi4 = jnp.concatenate([hi] + [p[:, :cells] for p in near], axis=1)
@@ -349,10 +357,11 @@
         for h in (0, 1):
             r = sl(h, half)
             grad_ref[r, :] = mm3(hi4[r], lo4[r], gl_hi[h], gl_lo[h])
-        if opening:
-            for later in range(1, steps):
-                force(later)
+
+        @pl.when(opening)
+        def _():
             choose()
+
         for piece in near_pieces + far_pieces:
             h, _, first, size = piece
             r = rows_of(piece)
@@ -364,21 +373,21 @@
             damp = damp_ref[step, r, cells:]
             x_ref[r, :cells] = damp * (x_ref[r, :cells] - depth * grad[:, :cells])
             x_ref[r, cells:] = damp * (x_ref[r, cells:] - depth * grad[:, cells:])
-            if not closing:
+
+            @pl.when(jnp.logical_not(closing))
+            def _():
                 shed(step + 1, piece)
                 div_copy(step + 1, piece).start()
 
-    lev_send[0] = elevation0
+
     for piece in far_pieces + near_pieces:
         shed(0, piece)
-    one_step(0, True, False)
-
-    def middle(step, _):
-        one_step(step, False, False)
+
+    def step_of(step, _):
+        one_step(step)
         return 0
 
-    lax.fori_loop(1, steps - 1, middle, 0)
-    one_step(steps - 1, False, True)
+    lax.fori_loop(0, steps, step_of, 0)
     migrate(1, *halves(x_ref[...]))
 
     def halo_sent(step, _):

time: 58.2 us -> 58.2 us (level)
  no operation moved by 1% of the time
where the time goes in v6:
time: 58.2 us; the launch traced here: 58 us
  Pallas kernels  57.3 us (98%)
  between operations  0.64 us (1%)
    pallas_call x1, Pallas kernels, local(): pl.pallas_call(functools.partial(kernel, n, slots), out_shape=(jax.ShapeD...  55 us
    pallas_call x1, Pallas kernels, local(): pl.pallas_call(functools.partial(settle, slots), out_shape=(jax.ShapeDtyp...  2.37 us

profile of v6, /device:TPU:0, one launch (start us, length us, event | category | flops | bytes accessed | tf_op | source)
XLA Modules:
  0.0 58.0 jit_solution(15973269915156779515)
XLA Ops:
  0.6 55.0 %surge.1 = (f32[32,16,128]{2,1,0:T(8,128)}, f32[32,16,256]{2,1,0:T(8,128)}) custom-call(f32[256,128]{1,0:T(8,128)} %elev_hbm.1, f32[512,128]{1,0:T(8,128)} %bitcast.13, f32[256,128]{1,0:T(8,128)} %depth_hbm.1, f32[256,128]{1,0:T(8,128)} %drag_hbm.1, f32[1280,128]{1,0:T(8,128)} %bitcast.10, f32[640,256]{1,0:T(8,128)} %bitcast.11, s32[4,256]{1,0:T(4,128)} %bitcast.17, ...), custom_call_target="tpu_custom_call" | custom-call | tf_op jit(solution)/shard_map/surge/pallas_call | solution.py:475
  55.6 2.4 %settle.1 = (f32[256,128]{1,0:T(8,128)}, f32[512,128]{1,0:T(8,128)}) custom-call(s32[1,256]{1,0:T(1,128)} %bitcast.16, f32[512,128]{1,0:T(8,128)} %bitcast.14, f32[512,256]{1,0:T(8,128)} %bitcast.12), custom_call_target="tpu_custom_call" | custom-call | tf_op jit(solution)/shard_map/settle/pallas_call | solution.py:550

commit v7 on v6

--- a/solution.py
+++ b/solution.py
@@ -43,7 +43,7 @@
     cells_ref, source_ref, series_ref, moved_ref,
     meta, gathered, x_ref, dl_hi, dl_lo, ds_both, gl_hi, gl_lo, gs_twice, gs_lo,
     damp_ref, depth_p, near_rows, near_cols, div_ref, grad_ref,
-    force_ref, relax_ref, div_send, div_recv, lev_send, lev_recv, pack, packed_level, packed_flow,
+    found_ref, rows_ref, columns_ref, force_ref, relax_ref, div_send, div_recv, lev_send, lev_recv, pack, packed_level, packed_flow,
     in_ss, meta_ss, meta_rs, div_ss, div_rs, lev_ss, lev_rs, mig_ss, mig_rs, own_ss,
 ):
     me = lax.axis_index("dom")
@@ -249,6 +249,15 @@
             damp_ref[s, :, :cells] = jnp.broadcast_to(mask, (blocks, cells))
             damp_ref[s, :, cells:] = mask * damping
 
+    def spread(values):
+        return lax.dot_general(
+            rows_ref[...], values, (((1,), (1,)), ((), ())), preferred_element_type=f32
+        )
+
+    def force(step):
+        hi, lo = halves(columns_ref[...] * found_ref[pl.ds(step, 1), :])
+        force_ref[step] = spread(hi) + spread(lo)
+
     def boundary():
         entries = cells_ref.shape[1]
         point = source_ref[...].astype(f32)
@@ -264,25 +273,17 @@
         rows = hot(iota((blocks, entries), 0) == block_place).astype(bf16)
         columns = hot(iota((cells, entries), 0) == element)
 
-        def spread(values):
-            return lax.dot_general(
-                rows, values, (((1,), (1,)), ((), ())), preferred_element_type=f32
-            )
-
+        rows_ref[...] = rows
+        columns_ref[...] = columns
         relax_ref[...] = relax_rate * spread(columns.astype(bf16))
 
         all_done(gathered, meta_rs)
         tall = meta.shape[0]
         hi, lo = halves(gathered[...].reshape(n * tall, width))
         found = (mm(hi, pick) + mm(lo, pick)).reshape(n, tall, entries)
-        found = jnp.sum(jnp.where(iota(found.shape, 0) == chunk[None], found, 0.0), axis=0)
-
-        def force(s):
-            hi, lo = halves(columns * found[s : s + 1])
-            force_ref[s] = spread(hi) + spread(lo)
-
-        force(0)
-        return force
+        found_ref[...] = jnp.sum(
+            jnp.where(iota(found.shape, 0) == chunk[None], found, 0.0), axis=0
+        )
 
     def choose():
         everyone = gathered[...]
@@ -321,9 +322,12 @@
         div_ref[...] = first[:, :cells] + (parts[:, :cells] + parts[:, cells:])
         @pl.when(opening)
         def _():
-            force = boundary()
-            for later in range(1, steps):
-                force(later)
+            boundary()
+            force(0)
+
+        @pl.when(step == min(1, steps - 1))
+        def _():
+            choose()
 
         for piece in near_pieces + far_pieces:
             h, _, first, size = piece
@@ -358,9 +362,9 @@
             r = sl(h, half)
             grad_ref[r, :] = mm3(hi4[r], lo4[r], gl_hi[h], gl_lo[h])
 
-        @pl.when(opening)
+        @pl.when(jnp.logical_not(closing))
         def _():
-            choose()
+            force(step + 1)
 
         for piece in near_pieces + far_pieces:
             h, _, first, size = piece
@@ -509,6 +513,9 @@
             vmem((blocks, 3 * blocks), bf16),
             vmem((blocks, cells), f32),
             vmem((blocks, wide), f32),
+            vmem((tall, boundary_cells.shape[0]), f32),
+            vmem((blocks, boundary_cells.shape[0]), bf16),
+            vmem((cells, boundary_cells.shape[0]), f32),
             vmem((steps, blocks, cells), f32),
             vmem((blocks, cells), f32),
             vmem((steps, 2, half, cells), f32),

time: 58.2 us -> 58 us (level)
  no operation moved by 1% of the time
where the time goes in v7:
time: 58 us; the launch traced here: 57.8 us
  Pallas kernels  57.1 us (98%)
  between operations  0.64 us (1%)
    pallas_call x1, Pallas kernels, local(): pl.pallas_call(functools.partial(kernel, n, slots), out_shape=(jax.ShapeD...  54.8 us
    pallas_call x1, Pallas kernels, local(): pl.pallas_call(functools.partial(settle, slots), out_shape=(jax.ShapeDtyp...  2.37 us

profile of v7, /device:TPU:0, one launch (start us, length us, event | category | flops | bytes accessed | tf_op | source)
XLA Modules:
  0.0 57.8 jit_solution(16670130073983377987)
XLA Ops:
  0.6 54.8 %surge.1 = (f32[32,16,128]{2,1,0:T(8,128)}, f32[32,16,256]{2,1,0:T(8,128)}) custom-call(f32[256,128]{1,0:T(8,128)} %elev_hbm.1, f32[512,128]{1,0:T(8,128)} %bitcast.13, f32[256,128]{1,0:T(8,128)} %depth_hbm.1, f32[256,128]{1,0:T(8,128)} %drag_hbm.1, f32[1280,128]{1,0:T(8,128)} %bitcast.10, f32[640,256]{1,0:T(8,128)} %bitcast.11, s32[4,256]{1,0:T(4,128)} %bitcast.17, ...), custom_call_target="tpu_custom_call" | custom-call | tf_op jit(solution)/shard_map/surge/pallas_call | solution.py:479
  55.4 2.4 %settle.1 = (f32[256,128]{1,0:T(8,128)}, f32[512,128]{1,0:T(8,128)}) custom-call(s32[1,256]{1,0:T(1,128)} %bitcast.16, f32[512,128]{1,0:T(8,128)} %bitcast.14, f32[512,256]{1,0:T(8,128)} %bitcast.12), custom_call_target="tpu_custom_call" | custom-call | tf_op jit(solution)/shard_map/settle/pallas_call | solution.py:557

commit v8 on v6

--- a/solution.py
+++ b/solution.py
@@ -89,11 +89,10 @@
     flips = [(1 - 2 * lax.rem(lax.div(me, 1 << k), 2)) * (1 << k) for k in range(bits)]
 
     def partner(i):
-        j = i - 1
-        m = lax.div(j + 1, 2) + (1 - lax.rem(j, 2)) * (n // 2)
+        m = i // 2 + (i % 2) * (n // 2)
         if n != 1 << bits:
             return lax.rem(me + m, n)
-        return me + sum(lax.rem(lax.div(m, 1 << k), 2) * flips[k] for k in range(bits))
+        return me + sum(flips[k] for k in range(bits) if m >> k & 1)
 
     def sl(k, size):
         return slice(k * size, (k + 1) * size)
@@ -197,11 +196,8 @@
         src = (packed_level, packed_flow)[kind]
         src[...] = (mm(pack[...], hi) + mm(pack[...], lo)).reshape(src.shape)
 
-        def send(i, _):
+        for i in range(1, n):
             state_copy(kind, partner(i), me).start()
-            return 0
-
-        lax.fori_loop(1, n, send, 0)
         own_copy(kind).start()
 
     moved = moved_ref[...].astype(f32)
@@ -215,11 +211,8 @@
         pl.semaphore_wait(barrier, n - 1)
 
     def send_tiles():
-        def send(i, _):
+        for i in range(1, n):
             tile_copy(partner(i), me).start()
-            return 0
-
-        lax.fori_loop(1, n, send, 0)
 
         def place(ids):
             return jnp.sum(jnp.where(sub == ids, pos_col, 0.0), axis=0, keepdims=True)

time: 58.2 us -> 58.1 us (level)
  no operation moved by 1% of the time
where the time goes in v8:
time: 58.1 us; the launch traced here: 57.9 us
  Pallas kernels  57.3 us (99%)
  between operations  0.64 us (1%)
    pallas_call x1, Pallas kernels, local(): pl.pallas_call(functools.partial(kernel, n, slots), out_shape=(jax.ShapeD...  54.9 us
    pallas_call x1, Pallas kernels, local(): pl.pallas_call(functools.partial(settle, slots), out_shape=(jax.ShapeDtyp...  2.37 us

profile of v8, /device:TPU:0, one launch (start us, length us, event | category | flops | bytes accessed | tf_op | source)
XLA Modules:
  0.0 57.9 jit_solution(14141606323917393101)
XLA Ops:
  0.6 54.9 %surge.1 = (f32[32,16,128]{2,1,0:T(8,128)}, f32[32,16,256]{2,1,0:T(8,128)}) custom-call(f32[256,128]{1,0:T(8,128)} %elev_hbm.1, f32[512,128]{1,0:T(8,128)} %bitcast.13, f32[256,128]{1,0:T(8,128)} %depth_hbm.1, f32[256,128]{1,0:T(8,128)} %drag_hbm.1, f32[1280,128]{1,0:T(8,128)} %bitcast.10, f32[640,256]{1,0:T(8,128)} %bitcast.11, s32[4,256]{1,0:T(4,128)} %bitcast.17, ...), custom_call_target="tpu_custom_call" | custom-call | tf_op jit(solution)/shard_map/surge/pallas_call | solution.py:468
  55.6 2.4 %settle.1 = (f32[256,128]{1,0:T(8,128)}, f32[512,128]{1,0:T(8,128)}) custom-call(s32[1,256]{1,0:T(1,128)} %bitcast.16, f32[512,128]{1,0:T(8,128)} %bitcast.14, f32[512,256]{1,0:T(8,128)} %bitcast.12), custom_call_target="tpu_custom_call" | custom-call | tf_op jit(solution)/shard_map/settle/pallas_call | solution.py:543
